TPU v7x, 128 devices: a whole 4x4x4 slice. The times are simulated.
128 devices in a mesh: occ: 8 (over y, core), va: 2 (over z_lo), vb: 8 (over x, z_hi).
Axes of the slice: x: 4, y: 4, z: 4 (z_hi: 2, z_lo: 2; z = z_hi * 2 + z_lo), core: 2. Of those that a mesh axis runs over, the one named last changes fastest.
Arguments:
- factors: float32 [24, 1024, 1408], P('occ', ('va', 'vb')), may hold values from -0.04 to 0.04
- eps_occ: float32 [24], P('occ'), may hold values from -2 to -0.4
- eps_vir: float32 [1024], P(('va', 'vb')), may hold values from 0.2 to 3
Outputs:
- pair_energy: float32 [24, 24], P('occ')
All inputs are finite; a program needn't handle non-finite values.
Results may differ from a plain program's by a relative error of at most 0.00007.
Values sent between devices are 32-bit elements; how exact they have to be, the bound alone decides.
A program may use at most 128 MiB of HBM per device.

v0:
```python
import jax
import jax.numpy as jnp
from jax import lax
from jax.sharding import PartitionSpec as P


def from_behind(value, axis, steps):
    count = lax.axis_size(axis)
    pairs = [(source, (source + steps) % count) for source in range(count)]
    return lax.ppermute(value, axis, pairs)


def on_device(factors, eps_occ, eps_vir):
    span = lax.axis_size("occ")
    group = lax.axis_index("occ")
    width = factors.shape[0]
    row_tile, row_eps = (
        lax.all_gather(factors, "vb", axis=1, tiled=True),
        lax.all_gather(eps_vir, "vb", axis=0, tiled=True),
    )
    col_tile, col_eps = (
        lax.all_gather(factors, "va", axis=1, tiled=True),
        lax.all_gather(eps_vir, "va", axis=0, tiled=True),
    )

    def integrals(visiting):
        return jnp.einsum("iap,jbp->ijab", row_tile, visiting, precision=lax.Precision.HIGHEST)

    direct = [None] * span
    visit_eps = [None] * span
    direct[0] = integrals(col_tile)
    visit_eps[0] = eps_occ
    carried = (col_tile, eps_occ)
    for stop in range(1, span):
        carried = from_behind((carried[0], carried[1]), "occ", 1)
        direct[stop] = integrals(carried[0])
        visit_eps[stop] = carried[1]
    mirrors = [direct[0]]
    for stop in range(1, span):
        mirrors.append(from_behind(direct[span - stop], "occ", stop))
    vir_sum = row_eps[:, None] + col_eps[None, :]
    energy = jnp.zeros((width, width * span), jnp.float32)
    for stop in range(span):
        tile = direct[stop]
        swapped = jnp.transpose(mirrors[stop], (1, 0, 2, 3))
        denom = (
            vir_sum[None, None, :, :]
            - eps_occ[:, None, None, None]
            - visit_eps[stop][None, :, None, None]
        )
        block = -jnp.sum(tile * (2.0 * tile - swapped) / denom, axis=(2, 3))
        start = (group - stop) % span * width
        energy = lax.dynamic_update_slice(energy, block, (jnp.int32(0), start))
    return lax.psum(energy, ("va", "vb"))


def solution(mesh):
    placed = (P("occ", ("va", "vb"), None), P("occ"), P(("va", "vb")))
    return jax.shard_map(
        on_device, mesh=mesh, in_specs=placed, out_specs=P("occ", None), check_vma=False
    )
```

profile of v0, /device:TPU:0, one launch (start us, length us, event | category | flops | bytes accessed | tf_op | source)
XLA Modules:
  0.0 564.4 jit_solution(1702234870563107978)
XLA Ops:
  8.0 40.0 %all-gather.3.cloned.1.call-done = f32[3,128,1408]{2,1,0:T(8,128)} async-done(((f32[3,64,1408]{2,1,0:T(8,128)}), f32[3,128,1408]{2,1,0:T(8,128)}) %all-gather.3.cloned.1.call-update) | async-done | bytes 2162704 | tf_op jit(solution)/shard_map/all_gather | solution.py:22
  48.0 27.6 %collective-permute-done = f32[3,128,1408]{2,1,0:T(8,128)S(1)} collective-permute-done((f32[3,128,1408]{2,1,0:T(8,128)}, f32[3,128,1408]{2,1,0:T(8,128)S(1)}, u32[]{:S(2)}, u32[]{:S(2)}) %collective-permute-start) | collective-permute-done | bytes 2162720 | tf_op jit(solution)/shard_map/ppermute | solution.py:10
  75.6 1.4 copy-done.8
  76.9 26.0 %collective-permute-done.1 = f32[3,128,1408]{2,1,0:T(8,128)S(1)} collective-permute-done((f32[3,128,1408]{2,1,0:T(8,128)S(1)}, f32[3,128,1408]{2,1,0:T(8,128)S(1)}, u32[]{:S(2)}, u32[]{:S(2)}) %collective-permute-start.1) | collective-permute-done | bytes 2162720 | tf_op jit(solution)/shard_map/ppermute | solution.py:10
  104.3 26.0 %collective-permute-done.2 = f32[3,128,1408]{2,1,0:T(8,128)S(1)} collective-permute-done((f32[3,128,1408]{2,1,0:T(8,128)S(1)}, f32[3,128,1408]{2,1,0:T(8,128)S(1)}, u32[]{:S(2)}, u32[]{:S(2)}) %collective-permute-start.2) | collective-permute-done | bytes 2162720 | tf_op jit(solution)/shard_map/ppermute | solution.py:10
  130.3 1.4 copy-done.4
  131.7 27.4 %collective-permute-done.3 = f32[3,128,1408]{2,1,0:T(8,128)S(1)} collective-permute-done((f32[3,128,1408]{2,1,0:T(8,128)S(1)}, f32[3,128,1408]{2,1,0:T(8,128)S(1)}, u32[]{:S(2)}, u32[]{:S(2)}) %collective-permute-start.3) | collective-permute-done | bytes 2162720 | tf_op jit(solution)/shard_map/ppermute | solution.py:10
  159.1 1.4 copy-done.6
  160.5 27.5 %collective-permute-done.4 = f32[3,128,1408]{2,1,0:T(8,128)} collective-permute-done((f32[3,128,1408]{2,1,0:T(8,128)S(1)}, f32[3,128,1408]{2,1,0:T(8,128)}, u32[]{:S(2)}, u32[]{:S(2)}) %collective-permute-start.4) | collective-permute-done | bytes 2162720 | tf_op jit(solution)/shard_map/ppermute | solution.py:10
  191.0 4.9 all-reduce.1
  195.9 23.9 %all-reduce = f32[512]{0:T(512)S(1)} all-reduce(f32[512]{0:T(512)S(1)} %dynamic-update-slice), channel_id=1, replica_groups=mesh['occ'=8,'va'=2,'vb'=8] {'vb'}, use_global_device_ids=true, to_apply=%add | all-reduce | flops 512 | bytes 4096
  220.1 4.2 collective-permute-done.10
  224.3 4.2 collective-permute-done.12
  228.5 4.2 collective-permute-done.14
  232.6 4.2 collective-permute-done.16
  236.8 15.8 %fusion.48 = f32[3,3,512,128]{2,3,0,1:T(8,128)S(1)} fusion(f32[3,512,1408]{2,1,0:T(8,128)} %all-gather.5.cloned.1.call-done, f32[3,128,1408]{2,1,0:T(8,128)} %copy-done.8), kind=kOutput, calls=%fused_computation.58 | convolution fusion | flops 9965666304 | bytes 13172736 | tf_op jit(solution)/shard_map/iap,jbp->ijab/dot_general | solution.py:27
  252.6 3.0 collective-permute-start.19
  255.6 13.6 %fusion.58 = f32[3,3,512,128]{2,3,0,1:T(8,128)S(1)} fusion(f32[3,512,1408]{2,1,0:T(8,128)S(1)} %copy-done, f32[3,128,1408]{2,1,0:T(8,128)} %copy-done.9), kind=kOutput, calls=%fused_computation.60 | convolution fusion | flops 9965666304 | bytes 13172736 | tf_op jit(solution)/shard_map/iap,jbp->ijab/dot_general | solution.py:27
  269.6 11.7 %fusion.53 = f32[3,3,512,128]{2,3,0,1:T(8,128)S(1)} fusion(f32[3,512,1408]{2,1,0:T(8,128)S(1)} %copy-done, f32[3,128,1408]{2,1,0:T(8,128)S(1)} %copy-done.5), kind=kOutput, calls=%fused_computation.59 | convolution fusion | flops 9965666304 | bytes 13172736 | tf_op jit(solution)/shard_map/iap,jbp->ijab/dot_general | solution.py:27
  281.4 11.6 %fusion.78 = f32[3,3,512,128]{2,3,1,0:T(8,128)S(1)} fusion(f32[3,512,1408]{2,1,0:T(8,128)S(1)} %copy-done, f32[3,128,1408]{2,1,0:T(8,128)S(1)} %copy-done.7), kind=kOutput, calls=%fused_computation.64 | convolution fusion | flops 9965666304 | bytes 13172736 | tf_op jit(solution)/shard_map/iap,jbp->ijab/dot_general | solution.py:27
  293.4 5.1 collective-permute-start.13
  298.5 21.7 %fusion.68 = f32[3,3,512,128]{2,3,1,0:T(8,128)} fusion(f32[3,512,1408]{2,1,0:T(8,128)S(1)} %copy-done, f32[3,128,1408]{2,1,0:T(8,128)} %collective-permute-done.5), kind=kOutput, calls=%fused_computation.62 | convolution fusion | flops 9965666304 | bytes 13172736 | tf_op jit(solution)/shard_map/iap,jbp->ijab/dot_general | solution.py:27
  320.2 21.9 %fusion.73 = f32[3,3,512,128]{2,3,1,0:T(8,128)} fusion(f32[3,512,1408]{2,1,0:T(8,128)S(1)} %copy-done, f32[3,128,1408]{2,1,0:T(8,128)} %collective-permute-done.4), kind=kOutput, calls=%fused_computation.63 | convolution fusion | flops 9965666304 | bytes 13172736 | tf_op jit(solution)/shard_map/iap,jbp->ijab/dot_general | solution.py:27
  342.1 30.6 %collective-permute-done.6 = f32[3,128,1408]{2,1,0:T(8,128)S(1)} collective-permute-done((f32[3,128,1408]{2,1,0:T(8,128)}, f32[3,128,1408]{2,1,0:T(8,128)S(1)}, u32[]{:S(2)}, u32[]{:S(2)}) %collective-permute-start.6) | collective-permute-done | bytes 2162720 | tf_op jit(solution)/shard_map/ppermute | solution.py:10
  372.8 13.1 %fusion.63 = f32[3,3,512,128]{2,3,1,0:T(8,128)} fusion(f32[3,512,1408]{2,1,0:T(8,128)S(1)} %copy-done, f32[3,128,1408]{2,1,0:T(8,128)S(1)} %collective-permute-done.6), kind=kOutput, calls=%fused_computation.61 | convolution fusion | flops 9965666304 | bytes 13172736 | tf_op jit(solution)/shard_map/iap,jbp->ijab/dot_general | solution.py:27
  386.3 11.8 %fusion.14 = f32[3,128,3,512]{3,1,2,0:T(8,128)S(1)} fusion(f32[3,512,1408]{2,1,0:T(8,128)S(1)} %copy-done, f32[3,128,1408]{2,1,0:T(8,128)S(1)} %copy-done.3), kind=kOutput, calls=%fused_computation.14 | convolution fusion | flops 9965666304 | bytes 13172736 | tf_op jit(solution)/shard_map/iap,jbp->ijab/dot_general | solution.py:27
  398.2 5.5 fusion.37
  403.9 35.9 %collective-permute-done.11 = f32[3,3,512,128]{2,3,1,0:T(8,128)} collective-permute-done((f32[3,3,512,128]{2,3,1,0:T(8,128)}, f32[3,3,512,128]{2,3,1,0:T(8,128)}, u32[]{:S(2)}, u32[]{:S(2)}) %collective-permute-start.11) | collective-permute-done | bytes 2359328 | tf_op jit(solution)/shard_map/ppermute | solution.py:10
  439.8 71.0 %collective-permute-done.9 = f32[3,3,512,128]{2,3,1,0:T(8,128)} collective-permute-done((f32[3,3,512,128]{2,3,1,0:T(8,128)}, f32[3,3,512,128]{2,3,1,0:T(8,128)}, u32[]{:S(2)}, u32[]{:S(2)}) %collective-permute-start.9) | collective-permute-done | bytes 2359328 | tf_op jit(solution)/shard_map/ppermute | solution.py:10
  510.8 3.0 collective-permute-done.7
  513.9 5.3 fusion.34
  521.1 36.0 %psum.7 = f32[3,24]{1,0:T(4,128)} all-reduce(f32[3,24]{1,0:T(4,128)S(1)} %dynamic_update_slice.31), channel_id=1, replica_groups=mesh['occ'=8,'va'=2,'vb'=8] {'va','vb'}, use_global_device_ids=true, to_apply=%region_8.9 | all-reduce | flops 72 | bytes 576 | tf_op jit(solution)/shard_map/psum | solution.py:54
  (85 shorter events, 8.0 us)
Async XLA Ops:
  6.5 181.5 %copy-start.13 = (u32[128]{0:T(128)S(1)}, u32[128]{0:T(128)}, u32[]{:S(2)}) copy-start(u32[128]{0:T(128)} %constant.86) | copy-start | bytes 1540
  6.5 182.1 %copy-start.12 = (u32[128]{0:T(128)S(1)}, u32[128]{0:T(128)}, u32[]{:S(2)}) copy-start(u32[128]{0:T(128)} %constant.81) | copy-start | bytes 1540
  6.5 213.4 %copy-start.10 = (f32[3]{0:T(128)S(1)}, f32[3]{0:T(128)}, u32[]{:S(2)}) copy-start(f32[3]{0:T(128)} %param.4) | copy-start | bytes 40
  6.5 184.0 %copy-start.11 = (f32[64]{0:T(128)S(1)}, f32[64]{0:T(128)}, u32[]{:S(2)}) copy-start(f32[64]{0:T(128)} %param.5) | copy-start | bytes 772
  6.5 41.4 %all-gather.3.cloned.1.call-start = ((), (), s32[]{:S(2)}) async-start(), calls=%async_computation | async-start | bytes 3244032 | tf_op jit(solution)/shard_map/all_gather | solution.py:22
  7.3 229.5 %all-gather.5.cloned.1.call-start = ((), (), s32[]{:S(2)}) async-start(), calls=%async_computation.1 | async-start | bytes 9732096 | tf_op jit(solution)/shard_map/all_gather | solution.py:18
  48.0 27.6 %collective-permute-start = (f32[3,128,1408]{2,1,0:T(8,128)}, f32[3,128,1408]{2,1,0:T(8,128)S(1)}, u32[]{:S(2)}, u32[]{:S(2)}) collective-permute-start(f32[3,128,1408]{2,1,0:T(8,128)} %all-gather.3.cloned.1.call-done), channel_id=1, source_target_pairs={{0,16},{16,32},{32,48},{48,64},{64,80},{80,96},{96,112},{112,0},{1... | collective-permute-start | bytes 6488072 | tf_op jit(solution)/shard_map/ppermute | solution.py:10
  75.6 27.4 %collective-permute-start.1 = (f32[3,128,1408]{2,1,0:T(8,128)S(1)}, f32[3,128,1408]{2,1,0:T(8,128)S(1)}, u32[]{:S(2)}, u32[]{:S(2)}) collective-permute-start(f32[3,128,1408]{2,1,0:T(8,128)S(1)} %collective-permute-done), channel_id=1, source_target_pairs={{0,16},{16,32},{32,48},{48,64},{64,80},{80,96},{96,112},{112,0},{1... | collective-permute-start | bytes 6488072 | tf_op jit(solution)/shard_map/ppermute | solution.py:10
  102.9 27.4 %collective-permute-start.2 = (f32[3,128,1408]{2,1,0:T(8,128)S(1)}, f32[3,128,1408]{2,1,0:T(8,128)S(1)}, u32[]{:S(2)}, u32[]{:S(2)}) collective-permute-start(f32[3,128,1408]{2,1,0:T(8,128)S(1)} %collective-permute-done.1), channel_id=1, source_target_pairs={{0,16},{16,32},{32,48},{48,64},{64,80},{80,96},{96,112},{112,0},{1... | collective-permute-start | bytes 6488072 | tf_op jit(solution)/shard_map/ppermute | solution.py:10
  131.7 27.4 %collective-permute-start.3 = (f32[3,128,1408]{2,1,0:T(8,128)S(1)}, f32[3,128,1408]{2,1,0:T(8,128)S(1)}, u32[]{:S(2)}, u32[]{:S(2)}) collective-permute-start(f32[3,128,1408]{2,1,0:T(8,128)S(1)} %collective-permute-done.2), channel_id=1, source_target_pairs={{0,16},{16,32},{32,48},{48,64},{64,80},{80,96},{96,112},{112,0},{1... | collective-permute-start | bytes 6488072 | tf_op jit(solution)/shard_map/ppermute | solution.py:10
  160.5 27.5 %collective-permute-start.4 = (f32[3,128,1408]{2,1,0:T(8,128)S(1)}, f32[3,128,1408]{2,1,0:T(8,128)}, u32[]{:S(2)}, u32[]{:S(2)}) collective-permute-start(f32[3,128,1408]{2,1,0:T(8,128)S(1)} %collective-permute-done.3), channel_id=1, source_target_pairs={{0,16},{16,32},{32,48},{48,64},{64,80},{80,96},{96,112},{112,0},{1... | collective-permute-start | bytes 6488072 | tf_op jit(solution)/shard_map/ppermute | solution.py:10
  188.0 81.3 %collective-permute-start.5 = (f32[3,128,1408]{2,1,0:T(8,128)}, f32[3,128,1408]{2,1,0:T(8,128)}, u32[]{:S(2)}, u32[]{:S(2)}) collective-permute-start(f32[3,128,1408]{2,1,0:T(8,128)} %collective-permute-done.4), channel_id=1, source_target_pairs={{0,16},{16,32},{32,48},{48,64},{64,80},{80,96},{96,112},{112,0},{1... | collective-permute-start | bytes 6488072 | tf_op jit(solution)/shard_map/ppermute | solution.py:10
  188.0 32.1 %collective-permute-start.8 = (f32[3]{0:T(128)}, f32[3]{0:T(128)S(1)}, u32[]{:S(2)}, u32[]{:S(2)}) collective-permute-start(f32[3]{0:T(128)} %param.4), channel_id=1, source_target_pairs={{0,16},{16,32},{32,48},{48,64},{64,80},{80,96},{96,112},{112,0},{1... | collective-permute-start | bytes 44 | tf_op jit(solution)/shard_map/ppermute | solution.py:10
  220.1 4.2 collective-permute-start.10
  224.3 4.2 collective-permute-start.12
  228.4 4.2 collective-permute-start.14
  232.6 4.2 collective-permute-start.16
  236.8 56.6 %collective-permute-start.18 = (f32[3]{0:T(128)S(1)}, f32[3]{0:T(128)S(1)}, u32[]{:S(2)}, u32[]{:S(2)}) collective-permute-start(f32[3]{0:T(128)S(1)} %collective-permute-done.16), channel_id=1, source_target_pairs={{0,16},{16,32},{32,48},{48,64},{64,80},{80,96},{96,112},{112,0},{1... | collective-permute-start | bytes 44 | tf_op jit(solution)/shard_map/ppermute | solution.py:10
  236.8 18.7 %copy-start = (f32[3,512,1408]{2,1,0:T(8,128)S(1)}, f32[3,512,1408]{2,1,0:T(8,128)}, u32[]{:S(2)}) copy-start(f32[3,512,1408]{2,1,0:T(8,128)} %all-gather.5.cloned.1.call-done) | copy-start | bytes 25952260
  252.6 17.0 %copy-start.5 = (f32[3,128,1408]{2,1,0:T(8,128)S(1)}, f32[3,128,1408]{2,1,0:T(8,128)}, u32[]{:S(2)}) copy-start(f32[3,128,1408]{2,1,0:T(8,128)} %copy-done.4) | copy-start | bytes 6488068
  252.6 133.3 %collective-permute-start.19 = (f32[3,3,512,128]{2,3,0,1:T(8,128)S(1)}, f32[3,3,512,128]{2,3,0,1:T(8,128)S(1)}, u32[]{:S(2)}, u32[]{:S(2)}) collective-permute-start(f32[3,3,512,128]{2,3,0,1:T(8,128)S(1)} %fusion.48), channel_id=1, source_target_pairs={{0,112},{16,0},{32,16},{48,32},{64,48},{80,64},{96,80},{112,96},{1... | collective-permute-start | bytes 7077896 | tf_op jit(solution)/shard_map/ppermute | solution.py:10
  269.2 12.1 %copy-start.1 = (f32[3,3,512,128]{2,3,0,1:T(8,128)}, f32[3,3,512,128]{2,3,0,1:T(8,128)S(1)}, u32[]{:S(2)}) copy-start(f32[3,3,512,128]{2,3,0,1:T(8,128)S(1)} %fusion.58) | copy-start | bytes 7077892
  269.2 12.2 %copy-start.7 = (f32[3,128,1408]{2,1,0:T(8,128)S(1)}, f32[3,128,1408]{2,1,0:T(8,128)}, u32[]{:S(2)}) copy-start(f32[3,128,1408]{2,1,0:T(8,128)} %copy-done.6) | copy-start | bytes 6488068
  269.2 116.7 %collective-permute-start.17 = (f32[3,3,512,128]{2,3,0,1:T(8,128)S(1)}, f32[3,3,512,128]{2,3,0,1:T(8,128)S(1)}, u32[]{:S(2)}, u32[]{:S(2)}) collective-permute-start(f32[3,3,512,128]{2,3,0,1:T(8,128)S(1)} %fusion.58), channel_id=1, source_target_pairs={{0,96},{16,112},{32,0},{48,16},{64,32},{80,48},{96,64},{112,80},{1... | collective-permute-start | bytes 7077896 | tf_op jit(solution)/shard_map/ppermute | solution.py:10
  269.3 103.4 %collective-permute-start.6 = (f32[3,128,1408]{2,1,0:T(8,128)}, f32[3,128,1408]{2,1,0:T(8,128)S(1)}, u32[]{:S(2)}, u32[]{:S(2)}) collective-permute-start(f32[3,128,1408]{2,1,0:T(8,128)} %collective-permute-done.5), channel_id=1, source_target_pairs={{0,16},{16,32},{32,48},{48,64},{64,80},{80,96},{96,112},{112,0},{1... | collective-permute-start | bytes 6488072 | tf_op jit(solution)/shard_map/ppermute | solution.py:10
  281.4 116.8 %collective-permute-start.15 = (f32[3,3,512,128]{2,3,0,1:T(8,128)S(1)}, f32[3,3,512,128]{2,3,0,1:T(8,128)S(1)}, u32[]{:S(2)}, u32[]{:S(2)}) collective-permute-start(f32[3,3,512,128]{2,3,0,1:T(8,128)S(1)} %fusion.53), channel_id=1, source_target_pairs={{0,80},{16,96},{32,112},{48,0},{64,16},{80,32},{96,48},{112,64},{1... | collective-permute-start | bytes 7077896 | tf_op jit(solution)/shard_map/ppermute | solution.py:10
  293.4 104.7 %collective-permute-start.13 = (f32[3,3,512,128]{2,3,1,0:T(8,128)S(1)}, f32[3,3,512,128]{2,3,1,0:T(8,128)S(1)}, u32[]{:S(2)}, u32[]{:S(2)}) collective-permute-start(f32[3,3,512,128]{2,3,1,0:T(8,128)S(1)} %fusion.78), channel_id=1, source_target_pairs={{0,64},{16,80},{32,96},{48,112},{64,0},{80,16},{96,32},{112,48},{1... | collective-permute-start | bytes 7077896 | tf_op jit(solution)/shard_map/ppermute | solution.py:10
  342.1 44.2 %copy-start.3 = (f32[3,128,1408]{2,1,0:T(8,128)S(1)}, f32[3,128,1408]{2,1,0:T(8,128)}, u32[]{:S(2)}) copy-start(f32[3,128,1408]{2,1,0:T(8,128)} %all-gather.3.cloned.1.call-done) | copy-start | bytes 6488068
  372.8 13.1 %collective-permute-start.20 = (f32[3]{0:T(128)S(1)}, f32[3]{0:T(128)S(1)}, u32[]{:S(2)}, u32[]{:S(2)}) collective-permute-start(f32[3]{0:T(128)S(1)} %collective-permute-done.18), channel_id=1, source_target_pairs={{0,16},{16,32},{32,48},{48,64},{64,80},{80,96},{96,112},{112,0},{1... | collective-permute-start | bytes 44 | tf_op jit(solution)/shard_map/ppermute | solution.py:10
  385.9 53.9 %collective-permute-start.11 = (f32[3,3,512,128]{2,3,1,0:T(8,128)}, f32[3,3,512,128]{2,3,1,0:T(8,128)}, u32[]{:S(2)}, u32[]{:S(2)}) collective-permute-start(f32[3,3,512,128]{2,3,1,0:T(8,128)} %fusion.73), channel_id=1, source_target_pairs={{0,48},{16,64},{32,80},{48,96},{64,112},{80,0},{96,16},{112,32},{1... | collective-permute-start | bytes 7077896 | tf_op jit(solution)/shard_map/ppermute | solution.py:10
  385.9 125.0 %collective-permute-start.9 = (f32[3,3,512,128]{2,3,1,0:T(8,128)}, f32[3,3,512,128]{2,3,1,0:T(8,128)}, u32[]{:S(2)}, u32[]{:S(2)}) collective-permute-start(f32[3,3,512,128]{2,3,1,0:T(8,128)} %fusion.68), channel_id=1, source_target_pairs={{0,32},{16,48},{32,64},{48,80},{64,96},{80,112},{96,0},{112,16},{1... | collective-permute-start | bytes 7077896 | tf_op jit(solution)/shard_map/ppermute | solution.py:10
  386.0 127.9 %collective-permute-start.7 = (f32[3,3,512,128]{2,3,1,0:T(8,128)}, f32[3,3,512,128]{2,3,1,0:T(8,128)}, u32[]{:S(2)}, u32[]{:S(2)}) collective-permute-start(f32[3,3,512,128]{2,3,1,0:T(8,128)} %fusion.63), channel_id=1, source_target_pairs={{0,16},{16,32},{32,48},{48,64},{64,80},{80,96},{96,112},{112,0},{1... | collective-permute-start | bytes 7077896 | tf_op jit(solution)/shard_map/ppermute | solution.py:10
  (5 other events, 17.2 us)
Sparse Core Ops, SparseCore 0:
  9.0 38.9 all-gather.2
  50.3 112.2 all-gather.4
where the time goes:
time: 571 us; the launch traced here: 564 us
  waiting for transfers between devices  334 us (58%)
  matrix products  121 us (21%)
  blocking collectives  64.9 us (11%)
  between operations  15.5 us (3%)
  other arithmetic  11.1 us (2%)
  local copies, waits for them, and re-layouts  9.18 us (2%)
  starting transfers between devices  8.98 us (2%)
    ppermute x21, waiting for transfers between devices, from_behind(): return lax.ppermute(value, axis, pairs)  292 us
    dot_general x8, matrix products, integrals(): jnp.einsum('iap,jbp->ijab', row_tile, visiting, precision=lax.Precision.H...  121 us
    all_gather x1, waiting for transfers between devices, on_device(): lax.all_gather(factors, 'va', axis=1, tiled=True)  40 us
    psum x1, blocking collectives, on_device(): return lax.psum(energy, ('va', 'vb'))  36 us
    unnamed x2, blocking collectives  28.8 us
  transfers between devices with their start and end apart: 23, of which 15 were waited for; matrix products, arithmetic and copies ran while one was open for 23% of the time, Pallas kernels for 0%

commit v1 on v0

v1 whole, which is shorter than its diff:
```python
import functools

import jax
import jax.numpy as jnp
from jax import lax
from jax.experimental import pallas as pl
from jax.experimental.pallas import tpu as pltpu
from jax.sharding import PartitionSpec as P

MESH = pl.DeviceIdType.MESH
STEPS = ((1, 0, 0), (3, 0, 0), (0, 1, 0), (0, 3, 0), (0, 0, 1), (0, 0, 3))
OCC, SUB, NAUX = 24, 16, 1408
ROWS = OCC * SUB

POINTS = ((0, 0, 0), (0, 0, 1), (1, 0, 0), (3, 0, 0), (0, 1, 1), (1, 3, 0), (1, 0, 3), (0, 0, 3), (1, 3, 1), (3, 1, 1), (2, 0, 3), (0, 2, 1))
HOPS = (
    (0, 0, -1, -1),
    (0, 1, -1, -1),
    (0, 3, -1, -1),
    (1, 0, 4, 0),
    (2, 0, 0, 0),
    (3, 0, 1, 0),
    (7, 0, 5, 0),
    (0, 2, -1, -1),
    (1, 3, 4, 0),
    (2, 3, 0, 0),
    (3, 3, 1, 0),
    (7, 3, 5, 0),
    (4, 0, 2, 1),
    (5, 0, 3, 2),
    (1, 1, 4, 0),
    (2, 1, 0, 0),
    (3, 1, 1, 0),
    (6, 0, 5, 2),
    (4, 3, 2, 1),
    (5, 3, 3, 2),
    (1, 2, 4, 0),
    (2, 2, 0, 0),
    (3, 2, 1, 0),
    (7, 2, 5, 0),
    (4, 1, 2, 1),
    (5, 1, 3, 2),
    (6, 1, 5, 2),
    (6, 3, 0, 7),
    (8, 0, 4, 5),
    (9, 0, 1, 4),
    (4, 2, 2, 1),
    (5, 2, 3, 2),
    (6, 2, 5, 2),
    (8, 3, 4, 5),
    (9, 3, 1, 4),
    (10, 0, 0, 6),
    (11, 0, 2, 4),
    (7, 1, 5, 0),
    (8, 1, 4, 5),
    (9, 1, 1, 4),
    (10, 1, 0, 6),
    (11, 3, 2, 4),
    (8, 2, 4, 5),
    (9, 2, 1, 4),
    (10, 2, 0, 6),
    (11, 1, 2, 4),
    (10, 3, 0, 6),
    (11, 2, 2, 4),
)
UPTO = (24, 24, 24, 36, 36, 36, 37, 41, 41, 41, 45, 45, 45, 47, 48, 48, 48, 48)
UNITS = (
    ((0, 0, 1), (0, 1, 2)),
    ((0, 2, 2), (1, 2, 2)),
    ((1, 3, 2), (2, 3, 1)),
    ((0, 4, 2), (1, 4, 2)),
    ((4, 3, 2), (0, 5, 2)),
    ((1, 5, 2), (4, 5, 2)),
    ((5, 3, 2), (6, 3, 2)),
    ((1, 6, 2), (4, 6, 2)),
    ((6, 5, 2), (7, 5, 2)),
    ((1, 7, 1), (7, 4, 2)),
    ((4, 8, 2), (8, 3, 2)),
    ((6, 9, 2), (2, 9, 2)),
    ((5, 9, 2), (8, 9, 1)),
    ((1, 10, 1), (5, 10, 2)),
    ((8, 10, 2), (0, 11, 2)),
    ((1, 11, 1), (7, 11, 1)),
    ((11, 6, 2), (11, 8, 2)),
    ((11, 10, 1), (11, 3, 2)),
)

SLOTS = len(POINTS)
CHILDREN = {}
for _slot, _part, _way, _from in HOPS:
    if _way >= 0:
        CHILDREN.setdefault((_from, _part), []).append((_slot, _way))
EPS_FROM = {slot: (source, way) for slot, part, way, source in HOPS if part == 0 and way >= 0}
READY = []
_seen = set()
for _pair in UNITS:
    _new = sorted({slot for unit in _pair for slot in unit[:2]} - _seen)
    _seen.update(_new)
    READY.append(_new)


def pick(step, core, field):
    value = jnp.int32(0)
    for index, pair in enumerate(UNITS):
        for side in range(2):
            if pair[side][field]:
                hit = (step == index) & (core == side)
                value = jnp.where(hit, jnp.int32(pair[side][field]), value)
    return value


def swap_pairs(rows, lane):
    rows = list(rows)
    for bit in (4, 2, 1):
        low = (lane // (16 * bit)) % 2 == 0
        for r in range(8):
            if r & bit:
                continue
            first, second = rows[r], rows[r + bit]
            rows[r] = jnp.where(low, first, pltpu.roll(second, 16 * bit, 1))
            rows[r + bit] = jnp.where(low, pltpu.roll(first, 128 - 16 * bit, 1), second)
    return rows


def kernel(
    eps_occ, eps_vir, b_ref, out_ref,
    held, high, low, tile, acc, evs, eo_block, eo_lane,
    hop_out, hop_in, sib_out, sib_in, row_out, row_in, ev_out, ev_in, eo_out, eo_in, own_sem,
):
    occ, va, vb = lax.axis_index("occ"), lax.axis_index("va"), lax.axis_index("vb")
    y, core = occ // 2, occ % 2
    x, z = vb // 2, (vb % 2) * 2 + va
    other = 1 - core

    def device(cx, cy, cz, ck):
        return (cy * 2 + ck, cz % 2, cx * 2 + cz // 2)

    sibling = device(x, y, z, other)

    def to_step(way):
        dx, dy, dz = STEPS[way]
        return device((x + 4 - dx) % 4, (y + 4 - dy) % 4, (z + 4 - dz) % 4, core)

    line = [(dy, dk) for dy in range(4) for dk in range(2) if (dy, dk) != (0, 0)]

    def line_device(dy, dk):
        return device(x, (y + dy) % 4, z, other if dk else core)

    barrier = pltpu.get_barrier_semaphore()
    partners = [to_step(way) for way in (0, 1, 4, 5)] + [line_device(dy, dk) for dy, dk in line]
    for partner in partners:
        pl.semaphore_signal(barrier, inc=1, device_id=partner, device_id_type=MESH)
    pl.semaphore_wait(barrier, len(partners))

    def piece(slot, part, half):
        start = ((y + POINTS[slot][1] + part) % 4) * 6
        return held.at[slot, pl.ds(start, 6), pl.ds(pl.multiple_of(half * 8, 8), 8), :]

    def row_copy(dy, dk):
        far = line_device(dy, dk)
        far_occ = far[0]
        return pltpu.make_async_remote_copy(
            src_ref=b_ref.at[:, pl.ds(pl.multiple_of(far_occ * 8, 8), 8), :],
            dst_ref=held.at[0, pl.ds(occ * 3, 3), pl.ds(pl.multiple_of((far_occ % 2) * 8, 8), 8), :],
            send_sem=row_out.at[dy, dk], recv_sem=row_in.at[dy, dk],
            device_id=far, device_id_type=MESH,
        )

    def row_arrival(dy, dk):
        near = line_device((4 - dy) % 4, dk)
        place = held.at[0, pl.ds(near[0] * 3, 3), pl.ds(pl.multiple_of(core * 8, 8), 8), :]
        return pltpu.make_async_remote_copy(
            src_ref=place, dst_ref=place, send_sem=row_out.at[dy, dk], recv_sem=row_in.at[dy, dk],
            device_id=near, device_id_type=MESH,
        )

    def sib_copy(slot, part):
        return pltpu.make_async_remote_copy(
            src_ref=piece(slot, part, core), dst_ref=piece(slot, part, core),
            send_sem=sib_out.at[slot, part], recv_sem=sib_in.at[slot, part],
            device_id=sibling, device_id_type=MESH,
        )

    def sib_arrival(slot, part):
        return pltpu.make_async_remote_copy(
            src_ref=piece(slot, part, other), dst_ref=piece(slot, part, other),
            send_sem=sib_out.at[slot, part], recv_sem=sib_in.at[slot, part],
            device_id=sibling, device_id_type=MESH,
        )

    def hop_copy(slot, part, way, source):
        return pltpu.make_async_remote_copy(
            src_ref=piece(source, part, core),
            dst_ref=held.at[
                slot,
                pl.ds(((y + POINTS[source][1] + part) % 4) * 6, 6),
                pl.ds(pl.multiple_of(core * 8, 8), 8),
                :,
            ],
            send_sem=hop_out.at[slot, part], recv_sem=hop_in.at[slot, part],
            device_id=to_step(way), device_id_type=MESH,
        )

    def hop_arrival(slot, part, way):
        return pltpu.make_async_remote_copy(
            src_ref=piece(slot, part, core), dst_ref=piece(slot, part, core),
            send_sem=hop_out.at[slot, part], recv_sem=hop_in.at[slot, part],
            device_id=to_step(way), device_id_type=MESH,
        )

    def ev_copy(slot, way, source):
        return pltpu.make_async_remote_copy(
            src_ref=evs.at[source], dst_ref=evs.at[slot], send_sem=ev_out.at[slot], recv_sem=ev_in.at[slot],
            device_id=to_step(way), device_id_type=MESH,
        )

    def eo_copy(dy, dk):
        return pltpu.make_async_remote_copy(
            src_ref=eo_block.at[pl.ds(occ * 3, 3)], dst_ref=eo_block.at[pl.ds(occ * 3, 3)],
            send_sem=eo_out.at[dy, dk], recv_sem=eo_in.at[dy, dk],
            device_id=line_device(dy, dk), device_id_type=MESH,
        )

    def eo_arrival(dy, dk):
        near = line_device((4 - dy) % 4, dk)
        place = eo_block.at[pl.ds(near[0] * 3, 3)]
        return pltpu.make_async_remote_copy(
            src_ref=place, dst_ref=place, send_sem=eo_out.at[dy, dk], recv_sem=eo_in.at[dy, dk],
            device_id=near, device_id_type=MESH,
        )

    own = pltpu.make_async_copy(
        b_ref.at[:, pl.ds(pl.multiple_of(occ * 8, 8), 8), :],
        held.at[0, pl.ds(occ * 3, 3), pl.ds(pl.multiple_of(core * 8, 8), 8), :],
        own_sem,
    )
    row_copy(0, 1).start()
    own.start()
    for dy, dk in line[1:]:
        if dy != 2:
            row_copy(dy, dk).start()
    for dk in range(2):
        row_copy(2, dk).start()

    lane = lax.broadcasted_iota(jnp.int32, (8, 128), 1)
    sub16 = lax.broadcasted_iota(jnp.int32, (16, 128), 0)
    down = jnp.zeros((16, 128), jnp.float32)
    across = jnp.zeros((8, 128), jnp.float32)
    for a in range(SUB):
        value = eps_vir[y * SUB + a]
        down = jnp.where(sub16 == a, value, down)
        across = jnp.where(lane % SUB == a, value, across)
    evs[0, :16, :] = down
    evs[0, 16:, :] = across
    for r in range(3):
        eo_block[occ * 3 + r] = jnp.full((8, 128), eps_occ[r], jnp.float32)
    for slot, (source, way) in EPS_FROM.items():
        if source == 0:
            ev_copy(slot, way, source).start()
    for dy, dk in line:
        eo_copy(dy, dk).start()
    acc[...] = jnp.zeros_like(acc)

    def event(slot, part, way):
        if slot == 0:
            dy = (4 - part) % 4
            for dk in range(2):
                if (dy, dk) == (0, 0):
                    own.wait()
                else:
                    row_arrival(dy, dk).wait_recv()
        else:
            hop_arrival(slot, part, way).wait_recv()
        for child, child_way in CHILDREN.get((slot, part), []):
            hop_copy(child, part, child_way, slot).start()
        sib_copy(slot, part).start()
        if part == 0 and slot:
            source, ev_way = EPS_FROM[slot]
            ev_copy(slot, ev_way, source).wait_recv()
            for child, (child_from, child_way) in EPS_FROM.items():
                if child_from == slot:
                    ev_copy(child, child_way, slot).start()

    def split(slot):
        def rows(i, carry):
            value = held[slot, i]
            top = value.astype(jnp.bfloat16)
            at = pl.ds(pl.multiple_of(i * SUB, SUB), SUB)
            high[slot, at, :] = top
            low[slot, at, :] = (value - top.astype(jnp.float32)).astype(jnp.bfloat16)
            return carry
        lax.fori_loop(0, OCC, rows, 0)

    contract = (((1,), (1,)), ((), ()))

    def step_body(step, split_done):
        split_upto = jnp.int32(0)
        total = 0
        for index in range(len(UNITS)):
            first = 0 if index == 0 else UPTO[index - 1]

            @pl.when(step == index)
            def _():
                for slot, part, way, _source in HOPS[first:UPTO[index]]:
                    event(slot, part, way)
                for slot in READY[index]:
                    for part in range(4):
                        sib_arrival(slot, part).wait_recv()
                if index == 0:
                    for dy, dk in line:
                        eo_arrival(dy, dk).wait_recv()
                    for block in range(3):
                        value = jnp.zeros((8, 128), jnp.float32)
                        for r in range(8):
                            value = jnp.where(lane // SUB == r, eo_block[block * 8 + r], value)
                        eo_lane[block] = value

            total += len(READY[index])
            split_upto = jnp.where(step == index, jnp.int32(total), split_upto)

        def one_split(index, carry):
            split(index)
            return carry

        lax.fori_loop(split_done, split_upto, one_split, 0)

        left, right = pick(step, core, 0), pick(step, core, 1)
        weight = pick(step, core, 2)
        scale = jnp.where(weight == 2, jnp.float32(0.5), jnp.float32(1.0))

        lh, ll, rh, rl = high[left], low[left], high[right], low[right]
        dot = functools.partial(lax.dot_general, dimension_numbers=contract, preferred_element_type=jnp.float32)
        tile[...] = dot(lh, rl) + dot(ll, rh) + dot(lh, rh)

        down = evs[left, :16, :] * scale
        across = evs[right, 16:, :]
        for block_j in range(3):
            lanes = pl.ds(block_j * 128, 128)
            row = across - eo_lane[block_j]
            for block_i in range(block_j + 1):
                mirror = swap_pairs(
                    [tile[(block_j * 8 + r) * SUB:(block_j * 8 + r + 1) * SUB, block_i * 128:block_i * 128 + 128] for r in range(8)],
                    lax.broadcasted_iota(jnp.int32, (SUB, 128), 1),
                )
                for r in range(8):
                    i = block_i * 8 + r
                    here = tile[i * SUB:(i + 1) * SUB, lanes]
                    shift = (row - eo_block[i]) * scale
                    denom = down + jnp.concatenate([shift, shift], axis=0)
                    guess = pl.reciprocal(denom, approx=True)
                    inverse = guess * (2.0 - denom * guess)
                    term = (here * (here - mirror[r]) + mirror[r] * mirror[r]) * inverse
                    acc[i, :, lanes] = acc[i, :, lanes] + (term[:8] + term[8:])
        return split_upto

    lax.fori_loop(0, len(UNITS), step_body, jnp.int32(0))

    group = (lax.broadcasted_iota(jnp.int32, (ROWS, 128), 0) // SUB == lax.broadcasted_iota(jnp.int32, (ROWS, 128), 1)).astype(jnp.float32)
    sums = lax.dot_general(
        jnp.sum(acc[...], axis=1), group, (((1,), (0,)), ((), ())),
        precision=lax.Precision.HIGHEST, preferred_element_type=jnp.float32,
    )
    out_ref[...] = -sums

    for dy, dk in line:
        row_copy(dy, dk).wait_send()
        eo_copy(dy, dk).wait_send()
    for slot, part, way, source in HOPS:
        sib_copy(slot, part).wait_send()
        if way >= 0:
            hop_copy(slot, part, way, source).wait_send()
    for slot, (source, way) in EPS_FROM.items():
        ev_copy(slot, way, source).wait_send()


def on_device(factors, eps_occ, eps_vir):
    f32, dma = jnp.float32, pltpu.SemaphoreType.DMA
    part = pl.pallas_call(
        kernel,
        out_shape=jax.ShapeDtypeStruct((OCC, 128), f32),
        in_specs=[
            pl.BlockSpec(memory_space=pltpu.SMEM),
            pl.BlockSpec(memory_space=pltpu.SMEM),
            pl.BlockSpec(memory_space=pltpu.VMEM),
        ],
        out_specs=pl.BlockSpec(memory_space=pltpu.VMEM),
        scratch_shapes=[
            pltpu.VMEM((SLOTS, OCC, SUB, NAUX), f32),
            pltpu.VMEM((SLOTS, ROWS, NAUX), jnp.bfloat16),
            pltpu.VMEM((SLOTS, ROWS, NAUX), jnp.bfloat16),
            pltpu.VMEM((ROWS, ROWS), f32),
            pltpu.VMEM((OCC, 8, ROWS), f32),
            pltpu.VMEM((SLOTS, 24, 128), f32),
            pltpu.VMEM((OCC, 8, 128), f32),
            pltpu.VMEM((3, 8, 128), f32),
            dma((SLOTS, 4)), dma((SLOTS, 4)),
            dma((SLOTS, 4)), dma((SLOTS, 4)),
            dma((4, 2)), dma((4, 2)),
            dma((SLOTS,)), dma((SLOTS,)),
            dma((4, 2)), dma((4, 2)),
            dma,
        ],
        compiler_params=pltpu.CompilerParams(
            collective_id=0, has_side_effects=True, vmem_limit_bytes=61 * 2**20
        ),
        cost_estimate=pl.CostEstimate(flops=45 * 10**9, bytes_accessed=2 * 10**6, transcendentals=0),
    )(eps_occ, eps_vir, factors)
    total = lax.psum(part[:, :OCC], ("occ", "va", "vb"))
    block = jnp.arange(OCC) // 8
    total = total + jnp.where(block[:, None] > block[None, :], total.T, 0.0)
    return lax.dynamic_slice_in_dim(total, lax.axis_index("occ") * 3, 3, 0)


def solution(mesh):
    placed = (P("occ", ("va", "vb"), None), P("occ"), P(("va", "vb")))
    return jax.shard_map(on_device, mesh=mesh, in_specs=placed, out_specs=P("occ", None), check_vma=False)
```

time: 571 us -> 176 us (0.31); the launches traced: 564 us -> 176 us
  waiting for transfers between devices: 334 us -> 0 us
  matrix products: 121 us -> 0 us
  Pallas kernels: 0 us -> 108 us
  between operations: 15.5 us -> 0.01 us
  other arithmetic: 11.1 us -> 0.65 us
  local copies, waits for them, and re-layouts: 9.18 us -> 0.15 us
  starting transfers between devices: 8.98 us -> 0 us
    ppermute x21 -> x0, waiting for transfers between devices: 292 us -> none  [from_behind(): return lax.ppermute(value, axis, pairs)]
    dot_general x8 -> x0, matrix products: 121 us -> none  [integrals(): jnp.einsum('iap,jbp->ijab', row_tile, visiting, precision=lax.Precision.H...]
    pallas_call x0 -> x1, Pallas kernels: none -> 108 us  [on_device(): pl.pallas_call(kernel, out_shape=jax.ShapeDtypeStruct((OCC, 128), f32), i...]
    all_gather x2 -> x0, waiting for transfers between devices: 40 us -> none  [the longest x1 40 us: on_device(): lax.all_gather(factors, 'va', axis=1, tiled=True)]
    psum x1, blocking collectives: 36 us -> 66.9 us  [on_device(): total = lax.psum(part[:, :OCC], ('occ', 'va', 'vb'))]
    unnamed x2 -> x0, blocking collectives: 28.8 us -> none
    reduce_sum x2 -> x0, other arithmetic: 10.8 us -> none  [on_device(): block = -jnp.sum(tile * (2.0 * tile - swapped) / denom, axis=(2, 3))]
    ppermute x21 -> x0, starting transfers between devices: 8.91 us -> none  [from_behind(): return lax.ppermute(value, axis, pairs)]
  transfers between devices with their start and end apart: 23 -> 0, of which waited for: 15 -> 0; matrix products, arithmetic and copies ran while one was open for 23% -> 0% of each run, Pallas kernels for 0% -> 0%
where the time goes in v1:
time: 176 us
  Pallas kernels  108 us (61%)
  blocking collectives  66.9 us (38%)
    pallas_call x1, Pallas kernels, on_device(): pl.pallas_call(kernel, out_shape=jax.ShapeDtypeStruct((OCC, 128), f32), i...  108 us
    psum x1, blocking collectives, on_device(): total = lax.psum(part[:, :OCC], ('occ', 'va', 'vb'))  66.9 us

profile of v1, /device:TPU:0, one launch (start us, length us, event | category | flops | bytes accessed | tf_op | source)
XLA Modules:
  0.0 175.5 jit_solution(6938946572756211891)
XLA Ops:
  0.0 0.1 dynamic-slice
  0.1 107.9 %shard_map.37 = f32[24,128]{1,0:T(8,128)} custom-call(f32[3]{0:T(128)} %eps_occ.1, f32[64]{0:T(128)} %eps_vir.1, f32[3,64,1408]{2,1,0:T(8,128)} %b_ref.1), custom_call_target="tpu_custom_call" | custom-call | flops 44999999488 | bytes 2000000 | tf_op jit(solution)/shard_map/pallas_call | solution.py:378
  107.9 66.9 %psum.7 = f32[24,24]{1,0:T(8,128)S(1)} all-reduce(f32[24,24]{1,0:T(8,128)} %bitcast.3), channel_id=1, replica_groups=mesh['occ'=8,'va'=2,'vb'=8] {'occ','va','vb'}, use_global_device_ids=true, to_apply=%region_0.0 | all-reduce | flops 576 | bytes 4608 | tf_op jit(solution)/shard_map/psum | solution.py:408
  174.8 0.1 copy.4
  174.9 0.7 dynamic-slice_add_fusion
  (1 shorter events, 0.0 us)

commit v2 on v1

--- a/solution.py
+++ b/solution.py
@@ -12,77 +12,81 @@
 OCC, SUB, NAUX = 24, 16, 1408
 ROWS = OCC * SUB
 
-POINTS = ((0, 0, 0), (0, 0, 1), (1, 0, 0), (3, 0, 0), (0, 1, 1), (1, 3, 0), (1, 0, 3), (0, 0, 3), (1, 3, 1), (3, 1, 1), (2, 0, 3), (0, 2, 1))
+POINTS = ((0, 0, 0), (0, 0, 1), (1, 0, 0), (0, 0, 3), (3, 0, 1), (0, 1, 0), (1, 3, 0), (0, 0, 2), (2, 3, 0), (3, 0, 2), (0, 2, 0), (2, 2, 0))
 HOPS = (
     (0, 0, -1, -1),
     (0, 1, -1, -1),
     (0, 3, -1, -1),
     (1, 0, 4, 0),
+    (3, 0, 5, 0),
     (2, 0, 0, 0),
-    (3, 0, 1, 0),
-    (7, 0, 5, 0),
     (0, 2, -1, -1),
+    (1, 1, 4, 0),
+    (3, 1, 5, 0),
+    (2, 1, 0, 0),
+    (4, 0, 1, 1),
+    (5, 0, 2, 0),
+    (6, 0, 3, 2),
     (1, 3, 4, 0),
+    (3, 3, 5, 0),
     (2, 3, 0, 0),
-    (3, 3, 1, 0),
-    (7, 3, 5, 0),
-    (4, 0, 2, 1),
-    (5, 0, 3, 2),
-    (1, 1, 4, 0),
-    (2, 1, 0, 0),
-    (3, 1, 1, 0),
-    (6, 0, 5, 2),
-    (4, 3, 2, 1),
-    (5, 3, 3, 2),
+    (4, 1, 1, 1),
+    (5, 1, 2, 0),
+    (6, 1, 3, 2),
     (1, 2, 4, 0),
+    (7, 0, 5, 3),
     (2, 2, 0, 0),
-    (3, 2, 1, 0),
-    (7, 2, 5, 0),
-    (4, 1, 2, 1),
-    (5, 1, 3, 2),
-    (6, 1, 5, 2),
-    (6, 3, 0, 7),
-    (8, 0, 4, 5),
-    (9, 0, 1, 4),
-    (4, 2, 2, 1),
-    (5, 2, 3, 2),
-    (6, 2, 5, 2),
-    (8, 3, 4, 5),
-    (9, 3, 1, 4),
-    (10, 0, 0, 6),
-    (11, 0, 2, 4),
-    (7, 1, 5, 0),
-    (8, 1, 4, 5),
-    (9, 1, 1, 4),
-    (10, 1, 0, 6),
-    (11, 3, 2, 4),
-    (8, 2, 4, 5),
-    (9, 2, 1, 4),
-    (10, 2, 0, 6),
-    (11, 1, 2, 4),
-    (10, 3, 0, 6),
-    (11, 2, 2, 4),
+    (4, 3, 1, 1),
+    (5, 3, 2, 0),
+    (6, 3, 3, 2),
+    (3, 2, 5, 0),
+    (8, 0, 0, 6),
+    (9, 0, 4, 4),
+    (4, 2, 1, 1),
+    (5, 2, 2, 0),
+    (6, 2, 3, 2),
+    (7, 1, 5, 3),
+    (7, 3, 4, 1),
+    (8, 1, 0, 6),
+    (10, 0, 2, 5),
+    (11, 0, 3, 8),
+    (7, 2, 4, 1),
+    (8, 3, 0, 6),
+    (9, 1, 1, 7),
+    (10, 1, 2, 5),
+    (11, 1, 3, 8),
+    (8, 2, 0, 6),
+    (9, 2, 4, 4),
+    (9, 3, 1, 7),
+    (10, 3, 2, 5),
+    (11, 3, 3, 8),
+    (10, 2, 2, 5),
+    (11, 2, 3, 8),
 )
-UPTO = (24, 24, 24, 36, 36, 36, 37, 41, 41, 41, 45, 45, 45, 47, 48, 48, 48, 48)
+UPTO = (
+    23, 23, 23, 28, 29, 29, 29, 34, 34, 34, 34, 36,
+    38, 39, 39, 39, 41, 43, 44, 44, 46, 46, 46, 46,
+    46, 48, 48, 48, 48, 48, 48, 48, 48, 48, 48, 48,
+)
 UNITS = (
-    ((0, 0, 1), (0, 1, 2)),
-    ((0, 2, 2), (1, 2, 2)),
-    ((1, 3, 2), (2, 3, 1)),
-    ((0, 4, 2), (1, 4, 2)),
-    ((4, 3, 2), (0, 5, 2)),
-    ((1, 5, 2), (4, 5, 2)),
-    ((5, 3, 2), (6, 3, 2)),
-    ((1, 6, 2), (4, 6, 2)),
-    ((6, 5, 2), (7, 5, 2)),
-    ((1, 7, 1), (7, 4, 2)),
-    ((4, 8, 2), (8, 3, 2)),
-    ((6, 9, 2), (2, 9, 2)),
-    ((5, 9, 2), (8, 9, 1)),
-    ((1, 10, 1), (5, 10, 2)),
-    ((8, 10, 2), (0, 11, 2)),
-    ((1, 11, 1), (7, 11, 1)),
-    ((11, 6, 2), (11, 8, 2)),
-    ((11, 10, 1), (11, 3, 2)),
+    ((0, 0, 1), (1, 0, 2)),
+    ((0, 2, 2), (2, 1, 2)),
+    ((3, 1, 1), (2, 3, 2)),
+    ((2, 4, 2), (4, 3, 2)),
+    ((0, 5, 2), (2, 5, 2)),
+    ((5, 1, 2), (5, 4, 2)),
+    ((5, 3, 2), (1, 6, 2)),
+    ((3, 6, 2), (6, 5, 2)),
+    ((4, 6, 2), (6, 7, 2)),
+    ((7, 5, 2), (8, 0, 2)),
+    ((5, 8, 1), (8, 7, 2)),
+    ((8, 3, 2), (8, 4, 2)),
+    ((5, 9, 2), (9, 2, 1)),
+    ((1, 10, 2), (10, 7, 1)),
+    ((9, 10, 2), (6, 10, 2)),
+    ((10, 4, 2), (0, 10, 1)),
+    ((4, 11, 2), (7, 11, 1)),
+    ((10, 11, 1), (1, 11, 2)),
 )
 
 SLOTS = len(POINTS)
@@ -124,8 +128,10 @@
 
 def kernel(
     eps_occ, eps_vir, b_ref, out_ref,
-    held, high, low, tile, acc, evs, eo_block, eo_lane,
+    held, both, tile, acc, evs, eo_block, eo_lane,
+    rows_out, rows_got, x_got, z_got,
     hop_out, hop_in, sib_out, sib_in, row_out, row_in, ev_out, ev_in, eo_out, eo_in, own_sem,
+    red_out, red_in, plane_out, plane_in,
 ):
     occ, va, vb = lax.axis_index("occ"), lax.axis_index("va"), lax.axis_index("vb")
     y, core = occ // 2, occ % 2
@@ -147,7 +153,9 @@
         return device(x, (y + dy) % 4, z, other if dk else core)
 
     barrier = pltpu.get_barrier_semaphore()
-    partners = [to_step(way) for way in (0, 1, 4, 5)] + [line_device(dy, dk) for dy, dk in line]
+    partners = [line_device(dy, dk) for dy, dk in line]
+    partners += [device((x + d) % 4, y, z, core) for d in range(1, 4)]
+    partners += [device(x, y, (z + d) % 4, core) for d in range(1, 4)]
     for partner in partners:
         pl.semaphore_signal(barrier, inc=1, device_id=partner, device_id_type=MESH)
     pl.semaphore_wait(barrier, len(partners))
@@ -286,8 +294,8 @@
             value = held[slot, i]
             top = value.astype(jnp.bfloat16)
             at = pl.ds(pl.multiple_of(i * SUB, SUB), SUB)
-            high[slot, at, :] = top
-            low[slot, at, :] = (value - top.astype(jnp.float32)).astype(jnp.bfloat16)
+            both[slot, at, :] = top
+            both[slot, pl.ds(pl.multiple_of(ROWS + i * SUB, SUB), SUB), :] = (value - top.astype(jnp.float32)).astype(jnp.bfloat16)
             return carry
         lax.fori_loop(0, OCC, rows, 0)
 
@@ -296,13 +304,16 @@
     def step_body(step, split_done):
         split_upto = jnp.int32(0)
         total = 0
+
+        def arrivals(index):
+            first = 0 if index == 0 else UPTO[index - 1]
+            for slot, part, way, _source in HOPS[first:UPTO[index]]:
+                event(slot, part, way)
+
         for index in range(len(UNITS)):
-            first = 0 if index == 0 else UPTO[index - 1]
-
             @pl.when(step == index)
             def _():
-                for slot, part, way, _source in HOPS[first:UPTO[index]]:
-                    event(slot, part, way)
+                arrivals(2 * index)
                 for slot in READY[index]:
                     for part in range(4):
                         sib_arrival(slot, part).wait_recv()
@@ -328,9 +339,15 @@
         weight = pick(step, core, 2)
         scale = jnp.where(weight == 2, jnp.float32(0.5), jnp.float32(1.0))
 
-        lh, ll, rh, rl = high[left], low[left], high[right], low[right]
         dot = functools.partial(lax.dot_general, dimension_numbers=contract, preferred_element_type=jnp.float32)
-        tile[...] = dot(lh, rl) + dot(ll, rh) + dot(lh, rh)
+        wide = dot(both[left, :ROWS], both[right])
+        tile[...] = wide[:, :ROWS] + wide[:, ROWS:]
+
+        for index in range(len(UNITS)):
+            if UPTO[2 * index] < UPTO[2 * index + 1]:
+                pl.when(step == index)(functools.partial(arrivals, 2 * index + 1))
+
+        tile[...] += dot(both[left, ROWS:], both[right, :ROWS])
 
         down = evs[left, :16, :] * scale
         across = evs[right, 16:, :]
@@ -355,13 +372,71 @@
 
     lax.fori_loop(0, len(UNITS), step_body, jnp.int32(0))
 
-    group = (lax.broadcasted_iota(jnp.int32, (ROWS, 128), 0) // SUB == lax.broadcasted_iota(jnp.int32, (ROWS, 128), 1)).astype(jnp.float32)
-    sums = lax.dot_general(
-        jnp.sum(acc[...], axis=1), group, (((1,), (0,)), ((), ())),
+    member = lax.broadcasted_iota(jnp.int32, (128, ROWS), 1) // SUB == lax.broadcasted_iota(jnp.int32, (128, ROWS), 0)
+    group = member.astype(jnp.float32)
+    summed = jnp.concatenate([jnp.sum(acc[...], axis=1), jnp.zeros((128 - OCC, ROWS), jnp.float32)], axis=0)
+    exact = functools.partial(
+        lax.dot_general, dimension_numbers=contract,
         precision=lax.Precision.HIGHEST, preferred_element_type=jnp.float32,
     )
-    out_ref[...] = -sums
-
+    upper, lower = exact(summed, group), exact(group, summed)
+    below = lax.broadcasted_iota(jnp.int32, (128, 128), 0) // 8 > lax.broadcasted_iota(jnp.int32, (128, 128), 1) // 8
+    pairs = upper + jnp.where(below, lower, 0.0)
+
+    rows_out[...] = jnp.zeros_like(rows_out)
+    for owner in range(8):
+        rows_out[owner, 0:3, :] = pairs[owner * 3:owner * 3 + 3, :]
+
+    def red_copy(dy, dk):
+        far = line_device(dy, dk)
+        return pltpu.make_async_remote_copy(
+            src_ref=rows_out.at[far[0]], dst_ref=rows_got.at[occ],
+            send_sem=red_out.at[dy, dk], recv_sem=red_in.at[dy, dk],
+            device_id=far, device_id_type=MESH,
+        )
+
+    def red_arrival(dy, dk):
+        near = line_device((4 - dy) % 4, dk)
+        return pltpu.make_async_remote_copy(
+            src_ref=rows_out.at[occ], dst_ref=rows_got.at[near[0]],
+            send_sem=red_out.at[dy, dk], recv_sem=red_in.at[dy, dk],
+            device_id=near, device_id_type=MESH,
+        )
+
+    for dy, dk in line:
+        red_copy(dy, dk).start()
+    rows_got[occ] = rows_out[occ]
+    for dy, dk in line:
+        red_arrival(dy, dk).wait_recv()
+    value = functools.reduce(lambda p, q: p + q, [rows_got[owner] for owner in range(8)])
+
+    sent = []
+    for axis, (place, got) in enumerate(((x, x_got), (z, z_got))):
+        got[place] = value
+        copies = []
+        for d in range(1, 4):
+            far = device((x + d) % 4, y, z, core) if axis == 0 else device(x, y, (z + d) % 4, core)
+            copy = pltpu.make_async_remote_copy(
+                src_ref=got.at[place], dst_ref=got.at[place],
+                send_sem=plane_out.at[axis, d], recv_sem=plane_in.at[axis, d],
+                device_id=far, device_id_type=MESH,
+            )
+            copy.start()
+            sent.append(copy)
+        for d in range(1, 4):
+            source = (place + 4 - d) % 4
+            pltpu.make_async_remote_copy(
+                src_ref=got.at[place], dst_ref=got.at[source],
+                send_sem=plane_out.at[axis, d], recv_sem=plane_in.at[axis, d],
+                device_id=far, device_id_type=MESH,
+            ).wait_recv()
+        value = (got[0] + got[1]) + (got[2] + got[3])
+    out_ref[...] = -value[:3, :OCC]
+
+    for copy in sent:
+        copy.wait_send()
+    for dy, dk in line:
+        red_copy(dy, dk).wait_send()
     for dy, dk in line:
         row_copy(dy, dk).wait_send()
         eo_copy(dy, dk).wait_send()
@@ -375,9 +450,9 @@
 
 def on_device(factors, eps_occ, eps_vir):
     f32, dma = jnp.float32, pltpu.SemaphoreType.DMA
-    part = pl.pallas_call(
+    return pl.pallas_call(
         kernel,
-        out_shape=jax.ShapeDtypeStruct((OCC, 128), f32),
+        out_shape=jax.ShapeDtypeStruct((3, OCC), f32),
         in_specs=[
             pl.BlockSpec(memory_space=pltpu.SMEM),
             pl.BlockSpec(memory_space=pltpu.SMEM),
@@ -386,29 +461,27 @@
         out_specs=pl.BlockSpec(memory_space=pltpu.VMEM),
         scratch_shapes=[
             pltpu.VMEM((SLOTS, OCC, SUB, NAUX), f32),
-            pltpu.VMEM((SLOTS, ROWS, NAUX), jnp.bfloat16),
-            pltpu.VMEM((SLOTS, ROWS, NAUX), jnp.bfloat16),
+            pltpu.VMEM((SLOTS, 2 * ROWS, NAUX), jnp.bfloat16),
             pltpu.VMEM((ROWS, ROWS), f32),
             pltpu.VMEM((OCC, 8, ROWS), f32),
             pltpu.VMEM((SLOTS, 24, 128), f32),
             pltpu.VMEM((OCC, 8, 128), f32),
             pltpu.VMEM((3, 8, 128), f32),
+            pltpu.VMEM((8, 8, 128), f32), pltpu.VMEM((8, 8, 128), f32),
+            pltpu.VMEM((4, 8, 128), f32), pltpu.VMEM((4, 8, 128), f32),
             dma((SLOTS, 4)), dma((SLOTS, 4)),
             dma((SLOTS, 4)), dma((SLOTS, 4)),
             dma((4, 2)), dma((4, 2)),
             dma((SLOTS,)), dma((SLOTS,)),
             dma((4, 2)), dma((4, 2)),
             dma,
+            dma((4, 2)), dma((4, 2)), dma((2, 4)), dma((2, 4)),
         ],
         compiler_params=pltpu.CompilerParams(
             collective_id=0, has_side_effects=True, vmem_limit_bytes=61 * 2**20
         ),
         cost_estimate=pl.CostEstimate(flops=45 * 10**9, bytes_accessed=2 * 10**6, transcendentals=0),
     )(eps_occ, eps_vir, factors)
-    total = lax.psum(part[:, :OCC], ("occ", "va", "vb"))
-    block = jnp.arange(OCC) // 8
-    total = total + jnp.where(block[:, None] > block[None, :], total.T, 0.0)
-    return lax.dynamic_slice_in_dim(total, lax.axis_index("occ") * 3, 3, 0)
 
 
 def solution(mesh):

time: 176 us -> 114 us (0.65)
  blocking collectives: 66.9 us -> 0 us
  Pallas kernels: 108 us -> 113 us
    psum x1 -> x0, blocking collectives: 66.9 us -> none  [on_device(): total = lax.psum(part[:, :OCC], ('occ', 'va', 'vb'))]
    pallas_call x1, Pallas kernels: 108 us -> 113 us  [on_device(): pl.pallas_call(kernel, out_shape=jax.ShapeDtypeStruct((3, OCC), f32), in_...]
where the time goes in v2:
time: 114 us
  Pallas kernels  113 us (99%)
  local copies, waits for them, and re-layouts  1.26 us (1%)
    pallas_call x1, Pallas kernels, on_device(): pl.pallas_call(kernel, out_shape=jax.ShapeDtypeStruct((3, OCC), f32), in_...  113 us

profile of v2, /device:TPU:0, one launch (start us, length us, event | category | flops | bytes accessed | tf_op | source)
XLA Modules:
  0.0 113.8 jit_solution(14021216116651347951)
XLA Ops:
  0.0 112.5 %shard_map.37 = f32[3,24]{1,0:T(4,128)} custom-call(f32[3]{0:T(128)} %eps_occ.1, f32[64]{0:T(128)} %eps_vir.1, f32[3,64,1408]{2,1,0:T(8,128)} %b_ref.1), custom_call_target="tpu_custom_call" | custom-call | flops 44999999488 | bytes 2000000 | tf_op jit(solution)/shard_map/pallas_call | solution.py:453
  112.5 1.3 %copy.5 = f32[3,24]{1,0:T(4,128)} copy(f32[3,24]{1,0:T(4,128)} %shard_map.37) | data formatting | bytes 576

commit v3 on v2

v3 whole, which is shorter than its diff:
```python
import functools

import jax
import jax.numpy as jnp
from jax import lax
from jax.experimental import pallas as pl
from jax.experimental.pallas import tpu as pltpu
from jax.sharding import PartitionSpec as P

MESH = pl.DeviceIdType.MESH
STEPS = ((1, 0, 0), (3, 0, 0), (0, 1, 0), (0, 3, 0), (0, 0, 1), (0, 0, 3))
OCC, SUB, NAUX = 24, 16, 1408
ROWS = OCC * SUB

POINTS = ((0, 0, 0), (0, 0, 3), (3, 0, 0), (1, 0, 0), (3, 0, 1), (0, 1, 0), (0, 3, 3), (2, 0, 0), (2, 0, 1), (0, 3, 2), (0, 2, 0), (0, 2, 2))
HOPS = (
    (0, 0, -1, -1),
    (0, 1, -1, -1),
    (0, 3, -1, -1),
    (1, 0, 5, 0),
    (3, 0, 0, 0),
    (2, 0, 1, 0),
    (0, 2, -1, -1),
    (1, 1, 5, 0),
    (3, 1, 0, 0),
    (2, 1, 1, 0),
    (4, 0, 4, 2),
    (5, 0, 2, 0),
    (6, 0, 3, 1),
    (1, 3, 5, 0),
    (3, 3, 0, 0),
    (2, 3, 1, 0),
    (4, 1, 4, 2),
    (5, 1, 2, 0),
    (6, 1, 3, 1),
    (1, 2, 5, 0),
    (7, 0, 0, 3),
    (2, 2, 1, 0),
    (4, 3, 4, 2),
    (5, 3, 2, 0),
    (6, 3, 3, 1),
    (9, 0, 5, 6),
    (3, 2, 0, 0),
    (7, 1, 1, 2),
    (4, 2, 4, 2),
    (5, 2, 2, 0),
    (6, 2, 3, 1),
    (9, 1, 5, 6),
    (7, 3, 0, 3),
    (8, 0, 1, 4),
    (8, 1, 4, 7),
    (10, 0, 2, 5),
    (11, 0, 3, 9),
    (9, 3, 5, 6),
    (7, 2, 0, 3),
    (8, 2, 1, 4),
    (8, 3, 4, 7),
    (10, 1, 2, 5),
    (11, 1, 3, 9),
    (9, 2, 5, 6),
    (10, 3, 2, 5),
    (11, 3, 3, 9),
    (10, 2, 2, 5),
    (11, 2, 3, 9),
)
UPTO = (
    22, 23, 23, 28, 29, 29, 31, 34, 34, 35, 37, 40,
    40, 41, 43, 44, 44, 44, 44, 46, 46, 46, 46, 46,
    48, 48, 48, 48, 48, 48, 48, 48, 48, 48, 48, 48,
)
UNITS = (
    ((0, 0, 1), (1, 0, 2)),
    ((2, 1, 2), (0, 2, 2)),
    ((3, 2, 1), (3, 1, 2)),
    ((3, 4, 2), (1, 4, 2)),
    ((2, 5, 2), (1, 5, 2)),
    ((3, 5, 2), (4, 5, 2)),
    ((5, 0, 2), (6, 5, 2)),
    ((2, 6, 2), (3, 6, 2)),
    ((4, 6, 2), (7, 5, 2)),
    ((6, 7, 2), (8, 5, 2)),
    ((1, 8, 1), (8, 6, 2)),
    ((4, 9, 2), (9, 5, 1)),
    ((9, 0, 2), (3, 9, 2)),
    ((4, 10, 2), (10, 6, 2)),
    ((3, 10, 2), (7, 10, 1)),
    ((10, 8, 2), (10, 0, 1)),
    ((11, 7, 1), (11, 3, 2)),
    ((11, 10, 1), (11, 4, 2)),
)

SLOTS = len(POINTS)
LAST = {slot: part for slot, part, _way, _from in HOPS}
CHILDREN = {}
for _slot, _part, _way, _from in HOPS:
    if _way >= 0:
        CHILDREN.setdefault((_from, _part), []).append((_slot, _way))
EPS_FROM = {slot: (source, way) for slot, part, way, source in HOPS if part == 0 and way >= 0}
READY = []
_seen = set()
for _pair in UNITS:
    _new = sorted({slot for unit in _pair for slot in unit[:2]} - _seen)
    _seen.update(_new)
    READY.append(_new)


PACK = 7


def words(core, field):
    out = []
    for start in range(0, len(UNITS), PACK):
        pair = [sum(u[side][field] << (4 * n) for n, u in enumerate(UNITS[start:start + PACK])) for side in range(2)]
        out.append(jnp.where(core == 0, jnp.int32(pair[0]), jnp.int32(pair[1])))
    return out


def pick(step, table):
    word = table[-1]
    for n in range(len(table) - 1, 0, -1):
        word = jnp.where(step < n * PACK, table[n - 1], word)
    return lax.shift_right_logical(word, 4 * lax.rem(step, PACK)) & 15


def swap_pairs(rows, lane):
    rows = list(rows)
    for bit in (4, 2, 1):
        low = (lane // (16 * bit)) % 2 == 0
        for r in range(8):
            if r & bit:
                continue
            first, second = rows[r], rows[r + bit]
            rows[r] = jnp.where(low, first, pltpu.roll(second, 16 * bit, 1))
            rows[r + bit] = jnp.where(low, pltpu.roll(first, 128 - 16 * bit, 1), second)
    return rows


def kernel(
    eps_occ, eps_vir, b_ref, out_ref,
    held, both, tile, done, acc, evs, eo_block, eo_lane,
    rows_out, rows_got, plane_got,
    hop_out, hop_in, sib_out, sib_in, row_out, row_in, ev_out, ev_in, eo_out, eo_in, own_sem,
    red_out, red_in, plane_out, plane_in,
):
    occ, va, vb = lax.axis_index("occ"), lax.axis_index("va"), lax.axis_index("vb")
    y, core = occ >> 1, occ & 1
    x, z = vb >> 1, (vb & 1) * 2 + va
    other = 1 - core

    def device(cx, cy, cz, ck):
        return (cy * 2 + ck, cz & 1, cx * 2 + (cz >> 1))

    xs, ys, zs = ([(place + d) & 3 for d in range(4)] for place in (x, y, z))
    sibling = device(x, y, z, other)
    near = [device(xs[(4 - dx) % 4], ys[(4 - dy) % 4], zs[(4 - dz) % 4], core) for dx, dy, dz in STEPS]
    quarter = [place * 6 for place in ys]
    half = (pl.multiple_of(core * 8, 8), pl.multiple_of(other * 8, 8))
    line = [(dy, dk) for dy in range(4) for dk in range(2) if (dy, dk) != (0, 0)]
    line_at = {(dy, dk): device(x, ys[dy], z, other if dk else core) for dy in range(4) for dk in range(2)}

    def to_step(way):
        return near[way]

    def line_device(dy, dk):
        return line_at[dy, dk]

    barrier = pltpu.get_barrier_semaphore()
    partners = [line_device(dy, dk) for dy, dk in line]
    partners += [device(xs[dx], y, zs[dz], core) for dx in range(4) for dz in range(4) if (dx, dz) != (0, 0)]
    for partner in partners:
        pl.semaphore_signal(barrier, inc=1, device_id=partner, device_id_type=MESH)
    pl.semaphore_wait(barrier, len(partners))

    def piece(slot, part, side):
        start = quarter[(POINTS[slot][1] + part) % 4]
        return held.at[slot, pl.ds(start, 6), pl.ds(half[side], 8), :]

    def row_copy(dy, dk):
        far = line_device(dy, dk)
        far_occ = far[0]
        return pltpu.make_async_remote_copy(
            src_ref=b_ref.at[:, pl.ds(pl.multiple_of(far_occ * 8, 8), 8), :],
            dst_ref=held.at[0, pl.ds(occ * 3, 3), pl.ds(half[dk], 8), :],
            send_sem=row_out.at[dy, dk], recv_sem=row_in.at[dy, dk],
            device_id=far, device_id_type=MESH,
        )

    def row_arrival(dy, dk):
        source = line_device((4 - dy) % 4, dk)
        place = held.at[0, pl.ds(source[0] * 3, 3), pl.ds(half[0], 8), :]
        return pltpu.make_async_remote_copy(
            src_ref=place, dst_ref=place, send_sem=row_out.at[dy, dk], recv_sem=row_in.at[dy, dk],
            device_id=source, device_id_type=MESH,
        )

    def sib_copy(slot, side):
        place = held.at[slot, :, pl.ds(half[side], 8), :]
        return pltpu.make_async_remote_copy(
            src_ref=place, dst_ref=place, send_sem=sib_out.at[slot], recv_sem=sib_in.at[slot],
            device_id=sibling, device_id_type=MESH,
        )

    def hop_copy(slot, part, way, source):
        return pltpu.make_async_remote_copy(
            src_ref=piece(source, part, 0),
            dst_ref=held.at[
                slot,
                pl.ds(quarter[(POINTS[source][1] + part) % 4], 6),
                pl.ds(half[0], 8),
                :,
            ],
            send_sem=hop_out.at[slot, part], recv_sem=hop_in.at[slot, part],
            device_id=to_step(way), device_id_type=MESH,
        )

    def hop_arrival(slot, part, way):
        return pltpu.make_async_remote_copy(
            src_ref=piece(slot, part, 0), dst_ref=piece(slot, part, 0),
            send_sem=hop_out.at[slot, part], recv_sem=hop_in.at[slot, part],
            device_id=to_step(way), device_id_type=MESH,
        )

    def ev_copy(slot, way, source):
        return pltpu.make_async_remote_copy(
            src_ref=evs.at[source], dst_ref=evs.at[slot], send_sem=ev_out.at[slot], recv_sem=ev_in.at[slot],
            device_id=to_step(way), device_id_type=MESH,
        )

    def eo_copy(dy, dk):
        return pltpu.make_async_remote_copy(
            src_ref=eo_block.at[pl.ds(occ * 3, 3)], dst_ref=eo_block.at[pl.ds(occ * 3, 3)],
            send_sem=eo_out.at[dy, dk], recv_sem=eo_in.at[dy, dk],
            device_id=line_device(dy, dk), device_id_type=MESH,
        )

    def eo_arrival(dy, dk):
        source = line_device((4 - dy) % 4, dk)
        place = eo_block.at[pl.ds(source[0] * 3, 3)]
        return pltpu.make_async_remote_copy(
            src_ref=place, dst_ref=place, send_sem=eo_out.at[dy, dk], recv_sem=eo_in.at[dy, dk],
            device_id=source, device_id_type=MESH,
        )

    own = pltpu.make_async_copy(
        b_ref.at[:, pl.ds(pl.multiple_of(occ * 8, 8), 8), :],
        held.at[0, pl.ds(occ * 3, 3), pl.ds(half[0], 8), :],
        own_sem,
    )
    row_copy(0, 1).start()
    own.start()
    for dy, dk in line[1:]:
        if dy != 2:
            row_copy(dy, dk).start()
    for dk in range(2):
        row_copy(2, dk).start()

    lane = lax.broadcasted_iota(jnp.int32, (8, 128), 1)
    sub16 = lax.broadcasted_iota(jnp.int32, (16, 128), 0)
    down = jnp.zeros((16, 128), jnp.float32)
    across = jnp.zeros((8, 128), jnp.float32)
    for a in range(SUB):
        value = eps_vir[y * SUB + a]
        down = jnp.where(sub16 == a, value, down)
        across = jnp.where(lane % SUB == a, value, across)
    evs[0, :16, :] = down
    evs[0, 16:, :] = across
    for r in range(3):
        eo_block[occ * 3 + r] = jnp.full((8, 128), eps_occ[r], jnp.float32)
    for slot, (source, way) in EPS_FROM.items():
        if source == 0:
            ev_copy(slot, way, source).start()
    for dy, dk in line:
        eo_copy(dy, dk).start()
    acc[...] = jnp.zeros_like(acc)
    done[...] = jnp.zeros_like(done)

    def event(slot, part, way):
        if slot == 0:
            dy = (4 - part) % 4
            for dk in range(2):
                if (dy, dk) == (0, 0):
                    own.wait()
                else:
                    row_arrival(dy, dk).wait_recv()
        else:
            hop_arrival(slot, part, way).wait_recv()
        for child, child_way in CHILDREN.get((slot, part), []):
            hop_copy(child, part, child_way, slot).start()
        if LAST[slot] == part:
            sib_copy(slot, 0).start()
        if part == 0 and slot:
            source, ev_way = EPS_FROM[slot]
            ev_copy(slot, ev_way, source).wait_recv()
            for child, (child_from, child_way) in EPS_FROM.items():
                if child_from == slot:
                    ev_copy(child, child_way, slot).start()

    def split(slot):
        def rows(i, carry):
            value = held[slot, i]
            top = value.astype(jnp.bfloat16)
            at = pl.ds(pl.multiple_of(i * SUB, SUB), SUB)
            both[slot, at, :] = top
            both[slot, pl.ds(pl.multiple_of(ROWS + i * SUB, SUB), SUB), :] = (value - top.astype(jnp.float32)).astype(jnp.bfloat16)
            return carry
        lax.fori_loop(0, OCC, rows, 0)

    contract = (((1,), (1,)), ((), ()))

    tables = [words(core, field) for field in range(3)]

    def energies(left, right, weight):
        scale = jnp.where(weight == 2, jnp.float32(0.5), jnp.float32(1.0))
        down = evs[left, :16, :] * scale
        across = evs[right, 16:, :]
        for block_j in range(3):
            lanes = pl.ds(block_j * 128, 128)
            row = across - eo_lane[block_j]
            for block_i in range(block_j + 1):
                mirror = swap_pairs(
                    [done[(block_j * 8 + r) * SUB:(block_j * 8 + r + 1) * SUB, block_i * 128:block_i * 128 + 128] for r in range(8)],
                    lax.broadcasted_iota(jnp.int32, (SUB, 128), 1),
                )
                for r in range(8):
                    i = block_i * 8 + r
                    here = done[i * SUB:(i + 1) * SUB, lanes]
                    shift = (row - eo_block[i]) * scale
                    denom = down + jnp.concatenate([shift, shift], axis=0)
                    guess = pl.reciprocal(denom, approx=True)
                    inverse = guess * (2.0 - denom * guess)
                    term = (here * (here - mirror[r]) + mirror[r] * mirror[r]) * inverse
                    acc[i, :, lanes] = acc[i, :, lanes] + (term[:8] + term[8:])

    def step_body(step, carry):
        split_done, old_left, old_right, old_weight = carry

        def arrivals(index):
            first = 0 if index == 0 else UPTO[index - 1]
            for slot, part, way, _source in HOPS[first:UPTO[index]]:
                event(slot, part, way)

        def before(index):
            arrivals(2 * index)
            for slot in READY[index]:
                sib_copy(slot, 1).wait_recv()
            if index == 0:
                for dy, dk in line:
                    eo_arrival(dy, dk).wait_recv()
                for block in range(3):
                    value = jnp.zeros((8, 128), jnp.float32)
                    for r in range(8):
                        value = jnp.where(lane // SUB == r, eo_block[block * 8 + r], value)
                    eo_lane[block] = value

        def between(index):
            arrivals(2 * index + 1)

        def choose(function, wanted):
            wanted = [index for index in range(len(UNITS)) if wanted(index)]
            for start in range(0, len(wanted), 4):
                some = wanted[start:start + 4]

                @pl.when((step >= some[0]) & (step <= some[-1]))
                def _():
                    for index in some:
                        pl.when(step == index)(functools.partial(function, index))

        choose(before, lambda index: READY[index] or UPTO[2 * index] > (UPTO[2 * index - 1] if index else 0))
        split_upto = jnp.int32(0)
        for index in range(len(UNITS)):
            if READY[index]:
                split_upto = split_upto + jnp.where(step >= index, jnp.int32(len(READY[index])), 0)

        def one_split(index, carry):
            split(index)
            return carry

        lax.fori_loop(split_done, split_upto, one_split, 0)

        left, right, weight = (pick(step, table) for table in tables)
        dot = functools.partial(lax.dot_general, dimension_numbers=contract, preferred_element_type=jnp.float32)
        wide = dot(both[left, :ROWS], both[right])
        tile[...] = wide[:, :ROWS] + wide[:, ROWS:]
        energies(old_left, old_right, old_weight)

        choose(between, lambda index: UPTO[2 * index] < UPTO[2 * index + 1])

        done[...] = tile[...] + dot(both[left, ROWS:], both[right, :ROWS])

        return split_upto, left, right, weight

    zero = jnp.int32(0)
    _, left, right, weight = lax.fori_loop(0, len(UNITS), step_body, (zero, zero, zero, zero))
    energies(left, right, weight)

    member = lax.broadcasted_iota(jnp.int32, (128, ROWS), 1) // SUB == lax.broadcasted_iota(jnp.int32, (128, ROWS), 0)
    group = member.astype(jnp.float32)
    summed = jnp.concatenate([jnp.sum(acc[...], axis=1), jnp.zeros((128 - OCC, ROWS), jnp.float32)], axis=0)
    exact = functools.partial(
        lax.dot_general, dimension_numbers=contract,
        precision=lax.Precision.HIGHEST, preferred_element_type=jnp.float32,
    )
    upper, lower = exact(summed, group), exact(group, summed)
    below = lax.broadcasted_iota(jnp.int32, (128, 128), 0) // 8 > lax.broadcasted_iota(jnp.int32, (128, 128), 1) // 8
    pairs = upper + jnp.where(below, lower, 0.0)

    rows_out[...] = jnp.zeros_like(rows_out)
    for owner in range(8):
        rows_out[owner, 0:3, :] = pairs[owner * 3:owner * 3 + 3, :]

    def red_copy(dy, dk):
        far = line_device(dy, dk)
        return pltpu.make_async_remote_copy(
            src_ref=rows_out.at[far[0]], dst_ref=rows_got.at[occ],
            send_sem=red_out.at[dy, dk], recv_sem=red_in.at[dy, dk],
            device_id=far, device_id_type=MESH,
        )

    def red_arrival(dy, dk):
        source = line_device((4 - dy) % 4, dk)
        return pltpu.make_async_remote_copy(
            src_ref=rows_out.at[occ], dst_ref=rows_got.at[source[0]],
            send_sem=red_out.at[dy, dk], recv_sem=red_in.at[dy, dk],
            device_id=source, device_id_type=MESH,
        )

    for dy, dk in line:
        red_copy(dy, dk).start()
    for slot in range(SLOTS):
        sib_copy(slot, 0).wait_send()
    for slot, part, way, source in HOPS:
        if way >= 0:
            hop_copy(slot, part, way, source).wait_send()
    rows_got[occ] = rows_out[occ]
    for dy, dk in line:
        red_arrival(dy, dk).wait_recv()
    value = functools.reduce(lambda p, q: p + q, [rows_got[owner] for owner in range(8)])

    place = x * 4 + z
    plane_got[place] = value
    plane = [(dx, dz) for dx in (2, 1, 3, 0) for dz in (2, 1, 3, 0) if (dx, dz) != (0, 0)]

    def plane_copy(dx, dz, to):
        far = device(xs[dx], y, zs[dz], core)
        return pltpu.make_async_remote_copy(
            src_ref=plane_got.at[place], dst_ref=plane_got.at[to],
            send_sem=plane_out.at[dx, dz], recv_sem=plane_in.at[dx, dz],
            device_id=far, device_id_type=MESH,
        )

    for dx, dz in plane:
        plane_copy(dx, dz, place).start()
    for slot, (source, way) in EPS_FROM.items():
        ev_copy(slot, way, source).wait_send()
    for dy, dk in line:
        row_copy(dy, dk).wait_send()
        eo_copy(dy, dk).wait_send()
        red_copy(dy, dk).wait_send()
    for dx, dz in plane:
        plane_copy(dx, dz, xs[(4 - dx) % 4] * 4 + zs[(4 - dz) % 4]).wait_recv()
    value = functools.reduce(lambda p, q: p + q, [plane_got[n] for n in range(16)])
    out_ref[...] = -value[:3, :OCC]
    for dx, dz in plane:
        plane_copy(dx, dz, place).wait_send()


def on_device(factors, eps_occ, eps_vir):
    f32, dma = jnp.float32, pltpu.SemaphoreType.DMA
    return pl.pallas_call(
        kernel,
        out_shape=jax.ShapeDtypeStruct((3, OCC), f32),
        in_specs=[
            pl.BlockSpec(memory_space=pltpu.SMEM),
            pl.BlockSpec(memory_space=pltpu.SMEM),
            pl.BlockSpec(memory_space=pltpu.VMEM),
        ],
        out_specs=pl.BlockSpec(memory_space=pltpu.VMEM),
        scratch_shapes=[
            pltpu.VMEM((SLOTS, OCC, SUB, NAUX), f32),
            pltpu.VMEM((SLOTS, 2 * ROWS, NAUX), jnp.bfloat16),
            pltpu.VMEM((ROWS, ROWS), f32), pltpu.VMEM((ROWS, ROWS), f32),
            pltpu.VMEM((OCC, 8, ROWS), f32),
            pltpu.VMEM((SLOTS, 24, 128), f32),
            pltpu.VMEM((OCC, 8, 128), f32),
            pltpu.VMEM((3, 8, 128), f32),
            pltpu.VMEM((8, 8, 128), f32), pltpu.VMEM((8, 8, 128), f32),
            pltpu.VMEM((16, 8, 128), f32),
            dma((SLOTS, 4)), dma((SLOTS, 4)),
            dma((SLOTS,)), dma((SLOTS,)),
            dma((4, 2)), dma((4, 2)),
            dma((SLOTS,)), dma((SLOTS,)),
            dma((4, 2)), dma((4, 2)),
            dma,
            dma((4, 2)), dma((4, 2)), dma((4, 4)), dma((4, 4)),
        ],
        compiler_params=pltpu.CompilerParams(
            collective_id=0, has_side_effects=True, vmem_limit_bytes=61 * 2**20
        ),
        cost_estimate=pl.CostEstimate(flops=45 * 10**9, bytes_accessed=2 * 10**6, transcendentals=0),
    )(eps_occ, eps_vir, factors)


def solution(mesh):
    placed = (P("occ", ("va", "vb"), None), P("occ"), P(("va", "vb")))
    return jax.shard_map(on_device, mesh=mesh, in_specs=placed, out_specs=P("occ", None), check_vma=False)
```

time: 114 us -> 103 us (0.904)
  Pallas kernels: 113 us -> 101 us
    pallas_call x1, Pallas kernels: 113 us -> 101 us  [on_device(): pl.pallas_call(kernel, out_shape=jax.ShapeDtypeStruct((3, OCC), f32), in_...]
where the time goes in v3:
time: 103 us; the launch traced here: 102 us
  Pallas kernels  101 us (98%)
  local copies, waits for them, and re-layouts  1.26 us (1%)
    pallas_call x1, Pallas kernels, on_device(): pl.pallas_call(kernel, out_shape=jax.ShapeDtypeStruct((3, OCC), f32), in_...  101 us

profile of v3, /device:TPU:0, one launch (start us, length us, event | category | flops | bytes accessed | tf_op | source)
XLA Modules:
  0.0 102.2 jit_solution(1304211380155172050)
XLA Ops:
  0.0 101.0 %shard_map.37 = f32[3,24]{1,0:T(4,128)} custom-call(f32[3]{0:T(128)} %eps_occ.1, f32[64]{0:T(128)} %eps_vir.1, f32[3,64,1408]{2,1,0:T(8,128)} %b_ref.1), custom_call_target="tpu_custom_call" | custom-call | flops 44999999488 | bytes 2000000 | tf_op jit(solution)/shard_map/pallas_call | solution.py:469
  101.0 1.3 %copy.5 = f32[3,24]{1,0:T(4,128)} copy(f32[3,24]{1,0:T(4,128)} %shard_map.37) | data formatting | bytes 576

commit v4 on v3

--- a/solution.py
+++ b/solution.py
@@ -90,7 +90,6 @@
 )
 
 SLOTS = len(POINTS)
-LAST = {slot: part for slot, part, _way, _from in HOPS}
 CHILDREN = {}
 for _slot, _part, _way, _from in HOPS:
     if _way >= 0:
@@ -137,7 +136,7 @@
 
 def kernel(
     eps_occ, eps_vir, b_ref, out_ref,
-    held, both, tile, done, acc, evs, eo_block, eo_lane,
+    held, both, done, acc, evs, eo_block, eo_lane,
     rows_out, rows_got, plane_got,
     hop_out, hop_in, sib_out, sib_in, row_out, row_in, ev_out, ev_in, eo_out, eo_in, own_sem,
     red_out, red_in, plane_out, plane_in,
@@ -193,10 +192,10 @@
             device_id=source, device_id_type=MESH,
         )
 
-    def sib_copy(slot, side):
-        place = held.at[slot, :, pl.ds(half[side], 8), :]
-        return pltpu.make_async_remote_copy(
-            src_ref=place, dst_ref=place, send_sem=sib_out.at[slot], recv_sem=sib_in.at[slot],
+    def sib_copy(slot, part, side):
+        return pltpu.make_async_remote_copy(
+            src_ref=piece(slot, part, side), dst_ref=piece(slot, part, side),
+            send_sem=sib_out.at[slot, part], recv_sem=sib_in.at[slot, part],
             device_id=sibling, device_id_type=MESH,
         )
 
@@ -286,8 +285,7 @@
             hop_arrival(slot, part, way).wait_recv()
         for child, child_way in CHILDREN.get((slot, part), []):
             hop_copy(child, part, child_way, slot).start()
-        if LAST[slot] == part:
-            sib_copy(slot, 0).start()
+        sib_copy(slot, part, 0).start()
         if part == 0 and slot:
             source, ev_way = EPS_FROM[slot]
             ev_copy(slot, ev_way, source).wait_recv()
@@ -335,14 +333,15 @@
         split_done, old_left, old_right, old_weight = carry
 
         def arrivals(index):
-            first = 0 if index == 0 else UPTO[index - 1]
+            first = 0 if index == 0 else UPTO[index - 2]
             for slot, part, way, _source in HOPS[first:UPTO[index]]:
                 event(slot, part, way)
 
         def before(index):
             arrivals(2 * index)
             for slot in READY[index]:
-                sib_copy(slot, 1).wait_recv()
+                for part in range(4):
+                    sib_copy(slot, part, 1).wait_recv()
             if index == 0:
                 for dy, dk in line:
                     eo_arrival(dy, dk).wait_recv()
@@ -352,9 +351,6 @@
                         value = jnp.where(lane // SUB == r, eo_block[block * 8 + r], value)
                     eo_lane[block] = value
 
-        def between(index):
-            arrivals(2 * index + 1)
-
         def choose(function, wanted):
             wanted = [index for index in range(len(UNITS)) if wanted(index)]
             for start in range(0, len(wanted), 4):
@@ -365,7 +361,7 @@
                     for index in some:
                         pl.when(step == index)(functools.partial(function, index))
 
-        choose(before, lambda index: READY[index] or UPTO[2 * index] > (UPTO[2 * index - 1] if index else 0))
+        choose(before, lambda index: READY[index] or UPTO[2 * index] > (UPTO[2 * index - 2] if index else 0))
         split_upto = jnp.int32(0)
         for index in range(len(UNITS)):
             if READY[index]:
@@ -380,13 +376,9 @@
         left, right, weight = (pick(step, table) for table in tables)
         dot = functools.partial(lax.dot_general, dimension_numbers=contract, preferred_element_type=jnp.float32)
         wide = dot(both[left, :ROWS], both[right])
-        tile[...] = wide[:, :ROWS] + wide[:, ROWS:]
+        narrow = dot(both[left, ROWS:], both[right, :ROWS])
         energies(old_left, old_right, old_weight)
-
-        choose(between, lambda index: UPTO[2 * index] < UPTO[2 * index + 1])
-
-        done[...] = tile[...] + dot(both[left, ROWS:], both[right, :ROWS])
-
+        done[...] = wide[:, :ROWS] + wide[:, ROWS:] + narrow
         return split_upto, left, right, weight
 
     zero = jnp.int32(0)
@@ -426,9 +418,8 @@
 
     for dy, dk in line:
         red_copy(dy, dk).start()
-    for slot in range(SLOTS):
-        sib_copy(slot, 0).wait_send()
     for slot, part, way, source in HOPS:
+        sib_copy(slot, part, 0).wait_send()
         if way >= 0:
             hop_copy(slot, part, way, source).wait_send()
     rows_got[occ] = rows_out[occ]
@@ -478,7 +469,7 @@
         scratch_shapes=[
             pltpu.VMEM((SLOTS, OCC, SUB, NAUX), f32),
             pltpu.VMEM((SLOTS, 2 * ROWS, NAUX), jnp.bfloat16),
-            pltpu.VMEM((ROWS, ROWS), f32), pltpu.VMEM((ROWS, ROWS), f32),
+            pltpu.VMEM((ROWS, ROWS), f32),
             pltpu.VMEM((OCC, 8, ROWS), f32),
             pltpu.VMEM((SLOTS, 24, 128), f32),
             pltpu.VMEM((OCC, 8, 128), f32),
@@ -486,7 +477,7 @@
             pltpu.VMEM((8, 8, 128), f32), pltpu.VMEM((8, 8, 128), f32),
             pltpu.VMEM((16, 8, 128), f32),
             dma((SLOTS, 4)), dma((SLOTS, 4)),
-            dma((SLOTS,)), dma((SLOTS,)),
+            dma((SLOTS, 4)), dma((SLOTS, 4)),
             dma((4, 2)), dma((4, 2)),
             dma((SLOTS,)), dma((SLOTS,)),
             dma((4, 2)), dma((4, 2)),

time: 103 us -> 98.8 us (0.959)
  Pallas kernels: 101 us -> 96.9 us
    pallas_call x1, Pallas kernels: 101 us -> 96.9 us  [on_device(): pl.pallas_call(kernel, out_shape=jax.ShapeDtypeStruct((3, OCC), f32), in_...]
where the time goes in v4:
time: 98.8 us; the launch traced here: 98.2 us
  Pallas kernels  96.9 us (98%)
  local copies, waits for them, and re-layouts  1.26 us (1%)
    pallas_call x1, Pallas kernels, on_device(): pl.pallas_call(kernel, out_shape=jax.ShapeDtypeStruct((3, OCC), f32), in_...  96.9 us

profile of v4, /device:TPU:0, one launch (start us, length us, event | category | flops | bytes accessed | tf_op | source)
XLA Modules:
  0.0 98.2 jit_solution(10753948570798937058)
XLA Ops:
  0.0 96.9 %shard_map.37 = f32[3,24]{1,0:T(4,128)} custom-call(f32[3]{0:T(128)} %eps_occ.1, f32[64]{0:T(128)} %eps_vir.1, f32[3,64,1408]{2,1,0:T(8,128)} %b_ref.1), custom_call_target="tpu_custom_call" | custom-call | flops 44999999488 | bytes 2000000 | tf_op jit(solution)/shard_map/pallas_call | solution.py:460
  96.9 1.3 %copy.5 = f32[3,24]{1,0:T(4,128)} copy(f32[3,24]{1,0:T(4,128)} %shard_map.37) | data formatting | bytes 576

commit v5 on v4

--- a/solution.py
+++ b/solution.py
@@ -463,7 +463,7 @@
         in_specs=[
             pl.BlockSpec(memory_space=pltpu.SMEM),
             pl.BlockSpec(memory_space=pltpu.SMEM),
-            pl.BlockSpec(memory_space=pltpu.VMEM),
+            pl.BlockSpec(memory_space=pl.ANY),
         ],
         out_specs=pl.BlockSpec(memory_space=pltpu.VMEM),
         scratch_shapes=[

time: 98.8 us -> 98.4 us (level)
  no operation moved by 1% of the time
where the time goes in v5:
time: 98.4 us; the launch traced here: 97.8 us
  Pallas kernels  96.5 us (98%)
  local copies, waits for them, and re-layouts  1.26 us (1%)
    pallas_call x1, Pallas kernels, on_device(): pl.pallas_call(kernel, out_shape=jax.ShapeDtypeStruct((3, OCC), f32), in_...  96.5 us

profile of v5, /device:TPU:0, one launch (start us, length us, event | category | flops | bytes accessed | tf_op | source)
XLA Modules:
  0.0 97.8 jit_solution(17694383109333285194)
XLA Ops:
  0.0 96.5 %shard_map.37 = f32[3,24]{1,0:T(4,128)} custom-call(f32[3]{0:T(128)} %eps_occ.1, f32[64]{0:T(128)} %eps_vir.1, f32[3,64,1408]{2,1,0:T(8,128)} %b_ref.1), custom_call_target="tpu_custom_call" | custom-call | flops 44999999488 | bytes 2000000 | tf_op jit(solution)/shard_map/pallas_call | solution.py:460
  96.5 1.3 %copy.5 = f32[3,24]{1,0:T(4,128)} copy(f32[3,24]{1,0:T(4,128)} %shard_map.37) | data formatting | bytes 576

commit v6 on v5

--- a/solution.py
+++ b/solution.py
@@ -418,29 +418,29 @@
 
     for dy, dk in line:
         red_copy(dy, dk).start()
+    rows_got[occ] = rows_out[occ]
+    for dy, dk in line:
+        red_arrival(dy, dk).wait_recv()
+    value = functools.reduce(lambda p, q: p + q, [rows_got[owner] for owner in range(8)])
+
+    place = x * 4 + z
+    plane_got[place] = value
+    plane = [(dx, dz) for dx in (2, 1, 3, 0) for dz in (2, 1, 3, 0) if (dx, dz) != (0, 0)]
+
+    def plane_copy(dx, dz, to):
+        far = device(xs[dx], y, zs[dz], core)
+        return pltpu.make_async_remote_copy(
+            src_ref=plane_got.at[place], dst_ref=plane_got.at[to],
+            send_sem=plane_out.at[dx, dz], recv_sem=plane_in.at[dx, dz],
+            device_id=far, device_id_type=MESH,
+        )
+
+    for dx, dz in plane:
+        plane_copy(dx, dz, place).start()
     for slot, part, way, source in HOPS:
         sib_copy(slot, part, 0).wait_send()
         if way >= 0:
             hop_copy(slot, part, way, source).wait_send()
-    rows_got[occ] = rows_out[occ]
-    for dy, dk in line:
-        red_arrival(dy, dk).wait_recv()
-    value = functools.reduce(lambda p, q: p + q, [rows_got[owner] for owner in range(8)])
-
-    place = x * 4 + z
-    plane_got[place] = value
-    plane = [(dx, dz) for dx in (2, 1, 3, 0) for dz in (2, 1, 3, 0) if (dx, dz) != (0, 0)]
-
-    def plane_copy(dx, dz, to):
-        far = device(xs[dx], y, zs[dz], core)
-        return pltpu.make_async_remote_copy(
-            src_ref=plane_got.at[place], dst_ref=plane_got.at[to],
-            send_sem=plane_out.at[dx, dz], recv_sem=plane_in.at[dx, dz],
-            device_id=far, device_id_type=MESH,
-        )
-
-    for dx, dz in plane:
-        plane_copy(dx, dz, place).start()
     for slot, (source, way) in EPS_FROM.items():
         ev_copy(slot, way, source).wait_send()
     for dy, dk in line:

time: 98.4 us -> 98.4 us (level)
  no operation moved by 1% of the time
where the time goes in v6:
time: 98.4 us; the launch traced here: 97.8 us
  Pallas kernels  96.5 us (98%)
  local copies, waits for them, and re-layouts  1.26 us (1%)
    pallas_call x1, Pallas kernels, on_device(): pl.pallas_call(kernel, out_shape=jax.ShapeDtypeStruct((3, OCC), f32), in_...  96.5 us

profile of v6, /device:TPU:0, one launch (start us, length us, event | category | flops | bytes accessed | tf_op | source)
XLA Modules:
  0.0 97.8 jit_solution(12885878337028838309)
XLA Ops:
  0.0 96.5 %shard_map.37 = f32[3,24]{1,0:T(4,128)} custom-call(f32[3]{0:T(128)} %eps_occ.1, f32[64]{0:T(128)} %eps_vir.1, f32[3,64,1408]{2,1,0:T(8,128)} %b_ref.1), custom_call_target="tpu_custom_call" | custom-call | flops 44999999488 | bytes 2000000 | tf_op jit(solution)/shard_map/pallas_call | solution.py:460
  96.5 1.3 %copy.5 = f32[3,24]{1,0:T(4,128)} copy(f32[3,24]{1,0:T(4,128)} %shard_map.37) | data formatting | bytes 576
